TPU v7x, 32 devices: a whole 2x2x4 slice. The times are simulated.
32 devices in a mesh: expert: 8 (over z, y), replica: 4 (over x, core).
Axes of the slice: x: 2, y: 2, z: 4, core: 2. Of those that a mesh axis runs over, the one named last changes fastest.
Arguments:
- tokens: bfloat16 [32768, 1024], P(('expert', 'replica')), may hold values from -6 to 6
- routes: int32 [32768, 1], P(('expert', 'replica')), may hold values from 0 to 7; in each aligned block of 1024 rows (0 to 1023, 1024 to 2047, ...) at most 256 rows name the same one
- gain_one: float32 [1024], replicated, may hold values from 0.5 to 1.5
- query_weight: bfloat16 [1024, 1024], replicated, may hold values from -0.1875 to 0.1875
- key_weight: bfloat16 [1024, 1024], replicated, may hold values from -0.1875 to 0.1875
- value_weight: bfloat16 [1024, 1024], replicated, may hold values from -0.1875 to 0.1875
- out_weight: bfloat16 [1024, 1024], replicated, may hold values from -1.5 to 1.5
- gain_two: float32 [1024], replicated, may hold values from 0.5 to 1.5
- up_weight: bfloat16 [8, 1024, 4096], P('expert'), may hold values from -0.1875 to 0.1875
- down_weight: bfloat16 [8, 4096, 1024], P('expert'), may hold values from -0.125 to 0.125
- cotangent: bfloat16 [32768, 1024], P(('expert', 'replica')), may hold values from -6 to 6
Outputs:
- output: bfloat16 [32768, 1024], P(('expert', 'replica'))
- grad_tokens: float32 [32768, 1024], P(('expert', 'replica'))
- grad_gain_one: float32 [1024], replicated
- grad_query_weight: float32 [1024, 1024], replicated
- grad_key_weight: float32 [1024, 1024], replicated
- grad_value_weight: float32 [1024, 1024], replicated
- grad_out_weight: float32 [1024, 1024], replicated
- grad_gain_two: float32 [1024], replicated
- grad_up_weight: float32 [8, 1024, 4096], P('expert')
- grad_down_weight: float32 [8, 4096, 1024], P('expert')
Inputs may be any that keep to these rules, and one draw needn't show every extreme that they name: `routes`: among the 1024 tokens of one device no expert is named more than 256 times; on some devices one is named exactly 256 times.
All inputs are finite; a program needn't handle non-finite values.
Results may differ from a plain program's by a relative error of at most 0.013.
Values may be sent and summed in bfloat16 or wider, within the bound.
A program may use at most 320 MiB of HBM per device.

v0:
```python
import jax
import jax.numpy as jnp
from jax import lax
from jax.sharding import PartitionSpec as P

HEAD_DIM = 64


epsilon = 1e-05


def layer_norm(rows, gain_vec):
    average = jnp.mean(rows, axis=-1, keepdims=True)
    centred = rows - average
    inverse = lax.rsqrt(jnp.mean(centred * centred, axis=-1, keepdims=True) + epsilon)
    normal = centred * inverse
    return (normal * gain_vec, normal, inverse)


def norm_back(grad_normed, gain_vec, normal, inverse):
    scaled = grad_normed * gain_vec
    centred = (
        scaled
        - jnp.mean(scaled, axis=-1, keepdims=True)
        - normal * jnp.mean(scaled * normal, axis=-1, keepdims=True)
    )
    return (centred * inverse, jnp.sum(grad_normed * normal, axis=0))


def project(left, right):
    return jnp.dot(left, right, preferred_element_type=jnp.float32)


def causal_scores(query_rows, key_heads, offset, scale_factor):
    block_rows = query_rows.shape[0]
    key_count = key_heads.shape[0]
    scores = (
        jnp.einsum("qhd,khd->hqk", query_rows, key_heads, preferred_element_type=jnp.float32)
        * scale_factor
    )
    row_ids = offset + lax.broadcasted_iota(jnp.int32, (block_rows, key_count), 0)
    col_ids = lax.broadcasted_iota(jnp.int32, (block_rows, key_count), 1)
    return jnp.where((col_ids <= row_ids)[None], scores, -1e30)


def attend_forward(query_heads, key_heads, value_heads, scale_factor):
    seq_len, head_count, head_size = query_heads.shape
    block_rows = min(512, seq_len)
    block_count = seq_len // block_rows
    query_blocks = query_heads.reshape(block_count, block_rows, head_count, head_size)

    def one_block(inputs):
        number, query_rows = inputs
        scores = causal_scores(query_rows, key_heads, number * block_rows, scale_factor)
        peak_score = jnp.max(scores, axis=-1, keepdims=True)
        exponent = jnp.exp(scores - peak_score)
        summed = jnp.sum(exponent, axis=-1, keepdims=True)
        softened = (exponent / summed).astype(jnp.bfloat16)
        attended = jnp.einsum(
            "hqk,khd->qhd", softened, value_heads, preferred_element_type=jnp.float32
        )
        return (attended.astype(jnp.bfloat16), (peak_score + jnp.log(summed))[..., 0])

    attended, log_totals = lax.map(
        one_block, (jnp.arange(block_count, dtype=jnp.int32), query_blocks)
    )
    return (attended.reshape(seq_len, head_count * head_size), log_totals)


def attend_backward(query_heads, key_heads, value_heads, log_totals, grad_attended, scale_factor):
    seq_len, head_count, head_size = query_heads.shape
    block_rows = min(512, seq_len)
    block_count = seq_len // block_rows
    query_blocks = query_heads.reshape(block_count, block_rows, head_count, head_size)
    grad_blocks = grad_attended.reshape(block_count, block_rows, head_count, head_size)

    def one_block(totals, inputs):
        number, query_rows, grad_rows, log_rows = inputs
        scores = causal_scores(query_rows, key_heads, number * block_rows, scale_factor)
        softened = jnp.exp(scores - log_rows[..., None])
        grad_values = totals[1] + jnp.einsum(
            "hqk,qhd->khd",
            softened.astype(jnp.bfloat16),
            grad_rows,
            preferred_element_type=jnp.float32,
        )
        grad_soft = jnp.einsum(
            "qhd,khd->hqk", grad_rows, value_heads, preferred_element_type=jnp.float32
        )
        grad_scores = softened * (grad_soft - jnp.sum(softened * grad_soft, axis=-1, keepdims=True))
        grad_scores = grad_scores.astype(jnp.bfloat16)
        grad_query = (
            jnp.einsum("hqk,khd->qhd", grad_scores, key_heads, preferred_element_type=jnp.float32)
            * scale_factor
        )
        grad_keys = (
            totals[0]
            + jnp.einsum(
                "hqk,qhd->khd", grad_scores, query_rows, preferred_element_type=jnp.float32
            )
            * scale_factor
        )
        return ((grad_keys, grad_values), grad_query)

    zeros_heads = jnp.zeros(key_heads.shape, jnp.float32)
    numbers = jnp.arange(block_count, dtype=jnp.int32)
    (grad_keys, grad_values), grad_query = lax.scan(
        one_block, (zeros_heads, zeros_heads), (numbers, query_blocks, grad_blocks, log_totals)
    )
    model_width = head_count * head_size
    return (
        grad_query.reshape(seq_len, model_width).astype(jnp.bfloat16),
        grad_keys.reshape(seq_len, model_width).astype(jnp.bfloat16),
        grad_values.reshape(seq_len, model_width).astype(jnp.bfloat16),
    )


def per_device(
    tokens,
    routes,
    gain_one,
    query_weight,
    key_weight,
    value_weight,
    out_weight,
    gain_two,
    up_weight,
    down_weight,
    cotangent,
):
    seq_len = tokens.shape[0]
    model_width = tokens.shape[1]
    head_count = model_width // HEAD_DIM
    groups = lax.axis_size("expert")
    capacity = 2 * seq_len // groups
    scale_factor = HEAD_DIM ** (-0.5)
    shape_heads = (seq_len, head_count, HEAD_DIM)
    residual = tokens.astype(jnp.float32)
    normed_one, normal_one, inverse_one = layer_norm(residual, gain_one)
    normed_low = normed_one.astype(jnp.bfloat16)
    query_heads = project(normed_low, query_weight).astype(jnp.bfloat16).reshape(shape_heads)
    key_heads = project(normed_low, key_weight).astype(jnp.bfloat16).reshape(shape_heads)
    value_heads = project(normed_low, value_weight).astype(jnp.bfloat16).reshape(shape_heads)
    attended, log_totals = attend_forward(query_heads, key_heads, value_heads, scale_factor)
    hidden_state = residual + project(attended, out_weight)
    normed_two, normal_two, inverse_two = layer_norm(hidden_state, gain_two)
    chosen = routes[:, 0]
    onehot = (chosen[:, None] == lax.broadcasted_iota(jnp.int32, (1, groups), 1)).astype(jnp.int32)
    rank_in = jnp.sum(jnp.cumsum(onehot, axis=0) * onehot, axis=1) - 1
    slot_index = chosen * capacity + rank_in
    slab_shape = (groups, capacity, model_width)
    flat_shape = (groups * capacity, model_width)
    outgoing = (
        jnp.zeros(flat_shape, jnp.bfloat16).at[slot_index].set(normed_two.astype(jnp.bfloat16))
    )
    arrived = lax.all_to_all(
        outgoing.reshape(slab_shape), "expert", split_axis=0, concat_axis=0, tiled=True
    ).reshape(flat_shape)
    up_matrix = up_weight[0]
    down_matrix = down_weight[0]
    hidden_pre = project(arrived, up_matrix)
    activated, gelu_back = jax.vjp(jax.nn.gelu, hidden_pre)
    activated_low = activated.astype(jnp.bfloat16)
    expert_result = project(activated_low, down_matrix).astype(jnp.bfloat16)
    returned = lax.all_to_all(
        expert_result.reshape(slab_shape), "expert", split_axis=0, concat_axis=0, tiled=True
    ).reshape(flat_shape)
    output = (hidden_state + returned[slot_index].astype(jnp.float32)).astype(jnp.bfloat16)
    grad_output = cotangent.astype(jnp.float32)
    grad_outgoing = jnp.zeros(flat_shape, jnp.bfloat16).at[slot_index].set(cotangent)
    grad_arrived = lax.all_to_all(
        grad_outgoing.reshape(slab_shape), "expert", split_axis=0, concat_axis=0, tiled=True
    ).reshape(flat_shape)
    grad_active = jnp.einsum(
        "rd,fd->rf", grad_arrived, down_matrix, preferred_element_type=jnp.float32
    )
    (grad_pre,) = gelu_back(grad_active)
    grad_pre_low = grad_pre.astype(jnp.bfloat16)
    grad_rows = jnp.einsum(
        "rf,df->rd", grad_pre_low, up_matrix, preferred_element_type=jnp.float32
    ).astype(jnp.bfloat16)
    grad_back = lax.all_to_all(
        grad_rows.reshape(slab_shape), "expert", split_axis=0, concat_axis=0, tiled=True
    ).reshape(flat_shape)
    grad_up_local = jnp.einsum(
        "rd,rf->df", arrived, grad_pre_low, preferred_element_type=jnp.float32
    )
    grad_down_local = jnp.einsum(
        "rf,rd->fd", activated_low, grad_arrived, preferred_element_type=jnp.float32
    )
    share_up, share_down = (
        lax.psum_scatter(
            grad_up_local[None].astype(jnp.bfloat16), "replica", scatter_dimension=2, tiled=True
        ).astype(jnp.float32),
        lax.psum_scatter(
            grad_down_local[None].astype(jnp.bfloat16), "replica", scatter_dimension=1, tiled=True
        ).astype(jnp.float32),
    )
    grad_up_weight, grad_down_weight = (
        lax.all_gather(share_up.astype(jnp.bfloat16), "replica", axis=2, tiled=True).astype(
            share_up.dtype
        ),
        lax.all_gather(share_down.astype(jnp.bfloat16), "replica", axis=1, tiled=True).astype(
            share_down.dtype
        ),
    )
    grad_normed_two = grad_back[slot_index].astype(jnp.float32)
    grad_norm_two, grad_gain_two = norm_back(grad_normed_two, gain_two, normal_two, inverse_two)
    grad_hidden = grad_output + grad_norm_two
    grad_hidden_low = grad_hidden.astype(jnp.bfloat16)
    grad_out_weight = jnp.einsum(
        "td,te->de", attended, grad_hidden_low, preferred_element_type=jnp.float32
    )
    grad_attended = jnp.einsum(
        "te,de->td", grad_hidden_low, out_weight, preferred_element_type=jnp.float32
    ).astype(jnp.bfloat16)
    grad_query, grad_keys, grad_values = attend_backward(
        query_heads,
        key_heads,
        value_heads,
        log_totals,
        grad_attended.reshape(shape_heads),
        scale_factor,
    )
    grad_query_weight = jnp.einsum(
        "td,te->de", normed_low, grad_query, preferred_element_type=jnp.float32
    )
    grad_key_weight = jnp.einsum(
        "td,te->de", normed_low, grad_keys, preferred_element_type=jnp.float32
    )
    grad_value_weight = jnp.einsum(
        "td,te->de", normed_low, grad_values, preferred_element_type=jnp.float32
    )
    grad_normed_one = jnp.einsum(
        "te,de->td", grad_query, query_weight, preferred_element_type=jnp.float32
    )
    grad_normed_one = grad_normed_one + jnp.einsum(
        "te,de->td", grad_keys, key_weight, preferred_element_type=jnp.float32
    )
    grad_normed_one = grad_normed_one + jnp.einsum(
        "te,de->td", grad_values, value_weight, preferred_element_type=jnp.float32
    )
    grad_norm_one, grad_gain_one = norm_back(grad_normed_one, gain_one, normal_one, inverse_one)
    grad_tokens = grad_hidden + grad_norm_one
    summed_dense = lax.psum(
        (
            grad_query_weight,
            grad_key_weight,
            grad_value_weight,
            grad_out_weight,
            grad_gain_one,
            grad_gain_two,
        ),
        ("expert", "replica"),
    )
    return (
        output,
        grad_tokens,
        summed_dense[4],
        summed_dense[0],
        summed_dense[1],
        summed_dense[2],
        summed_dense[3],
        summed_dense[5],
        grad_up_weight,
        grad_down_weight,
    )


def solution(mesh):
    placed = (
        P(("expert", "replica"), None),
        P(("expert", "replica"), None),
        P(),
        P(),
        P(),
        P(),
        P(),
        P(),
        P("expert", None, None),
        P("expert", None, None),
        P(("expert", "replica"), None),
    )
    return jax.shard_map(
        per_device,
        mesh=mesh,
        in_specs=placed,
        out_specs=(
            P(("expert", "replica"), None),
            P(("expert", "replica"), None),
            P(),
            P(),
            P(),
            P(),
            P(),
            P(),
            P("expert", None, None),
            P("expert", None, None),
        ),
        check_vma=False,
    )
```

profile of v0, /device:TPU:0, one launch (start us, length us, event | category | flops | bytes accessed | tf_op | source)
XLA Modules:
  0.0 1284.8 jit_solution(17676164135093944050)
XLA Ops:
  45.9 97.7 %while.27 = (s32[]{:T(128)}, bf16[2,512,16,64]{1,3,2,0:T(8,128)(2,1)}, f32[2,16,512]{2,1,0:T(8,128)S(1)}, s32[2]{0:T(128)S(1)}, bf16[2,512,16,64]{1,3,2,0:T(8,12...) while((s32[]{:T(128)}, ...), condition=%wide.region_5.6_spmd, body=%wide.region_2.5_spmd.sunk | while | flops 2249187840 | bytes 134484176 | solution.py:64
  48.0 15.6 %fusion.143 = (f32[16,512]{1,0:T(8,128)S(1)}, f32[16,512,1024]{2,1,0:T(8,128)}) fusion(pred[512,1024]{1,0:T(8,128)(4,1)S(1)} %iota_compare_fusion.6, bf16[1024,16,64]{0,2,1:T(8,128)(2,1)} %get-tuple-element.386, bf16[2,512,16,64]{1,3,2,0:T(8,128)(2,1)} %get-tuple-element.385, s32[]{:T(128)S(6)} %copy.58), kind=kOutput, calls=%fused_computation.7.clone.1 | convolution fusion | flops 1098899456 | bytes 37257220 | tf_op jit(solution)/shard_map/while/body/eval_jaxpr/qhd,khd->hqk/dot_general | solution.py:38
  96.5 15.6 %fusion.143 = (f32[16,512]{1,0:T(8,128)S(1)}, f32[16,512,1024]{2,1,0:T(8,128)}) fusion(pred[512,1024]{1,0:T(8,128)(4,1)S(1)} %iota_compare_fusion.6, bf16[1024,16,64]{0,2,1:T(8,128)(2,1)} %get-tuple-element.386, bf16[2,512,16,64]{1,3,2,0:T(8,128)(2,1)} %get-tuple-element.385, s32[]{:T(128)S(6)} %copy.58), kind=kOutput, calls=%fused_computation.7.clone.1 | convolution fusion | flops 1098899456 | bytes 37257220 | tf_op jit(solution)/shard_map/while/body/eval_jaxpr/qhd,khd->hqk/dot_general | solution.py:38
  183.9 84.6 %all-to-all-done = bf16[8,256,1024]{2,1,0:T(8,128)(2,1)} async-done(((bf16[8,256,1024]{2,1,0:T(8,128)(2,1)}), bf16[8,256,1024]{2,1,0:T(8,128)(2,1)}, u32[]{:S(2)}, u32[]{:S(2)}) %all-to-all-start) | async-done | bytes 4194336 | tf_op jit(solution)/shard_map/all_to_all | solution.py:156
  273.1 25.0 %fusion.46 = f32[2048,4096]{1,0:T(8,128)} fusion(bf16[2048,1024]{1,0:T(8,128)(2,1)} %bitcast.13, bf16[1,1024,4096]{2,1,0:T(8,128)(2,1)} %param.23), kind=kOutput, calls=%fused_computation.65 | convolution fusion | flops 17179869184 | bytes 46137344 | tf_op jit(solution)/shard_map/dot_general | solution.py:31
  298.2 67.5 %all-to-all-done.2 = bf16[8,256,1024]{2,1,0:T(8,128)(2,1)} async-done(((bf16[8,256,1024]{2,1,0:T(8,128)(2,1)}), bf16[8,256,1024]{2,1,0:T(8,128)(2,1)}, u32[]{:S(2)}, u32[]{:S(2)}) %all-to-all-start.2) | async-done | bytes 4194336 | tf_op jit(solution)/shard_map/all_to_all | solution.py:171
  365.6 44.9 %fusion.40 = bf16[2048,4096]{1,0:T(8,128)(2,1)} fusion(f32[2048,4096]{1,0:T(8,128)} %fusion.46, bf16[2048,1024]{1,0:T(8,128)(2,1)} %bitcast.19, bf16[1,4096,1024]{2,1,0:T(8,128)(2,1)} %param.24), kind=kOutput, calls=%fused_computation.58 | convolution fusion | flops 17347641344 | bytes 62914560 | tf_op jit(solution)/shard_map/rd,fd->rf/dot_general | solution.py:174
  410.5 23.4 %convert_bitcast_fusion.1 = bf16[1,1024,4096]{2,1,0:T(8,128)(2,1)} fusion(bf16[2048,1024]{1,0:T(8,128)(2,1)} %bitcast.13, bf16[2048,4096]{1,0:T(8,128)(2,1)} %fusion.40), kind=kOutput, calls=%fused_computation.68 | convolution fusion | flops 17184063488 | bytes 29360128 | tf_op jit(solution)/shard_map/rd,rf->df/dot_general | solution.py:185
  434.0 31.7 %convert_bitcast_fusion = bf16[1,4096,1024]{2,1,0:T(8,128)(2,1)} fusion(bf16[2048,1024]{1,0:T(8,128)(2,1)} %bitcast.19, f32[2048,4096]{1,0:T(8,128)} %fusion.46), kind=kOutput, calls=%fused_computation.67 | convolution fusion | flops 17259560960 | bytes 46137344 | tf_op jit(solution)/shard_map/rf,rd->fd/dot_general | solution.py:188
  465.7 28.8 %fusion.72 = bf16[2048,1024]{1,0:T(8,128)(2,1)} fusion(bf16[1,4096,1024]{2,1,0:T(8,128)(2,1)} %param.24, f32[2048,4096]{1,0:T(8,128)} %fusion.46), kind=kOutput, calls=%fused_computation.101 | convolution fusion | flops 17257463808 | bytes 46137344 | tf_op jit(solution)/shard_map/dot_general | solution.py:31
  504.8 23.8 %fusion.69 = bf16[2048,1024]{1,0:T(8,128)(2,1)} fusion(bf16[2048,4096]{1,0:T(8,128)(2,1)} %fusion.40, bf16[1,1024,4096]{2,1,0:T(8,128)(2,1)} %param.23), kind=kOutput, calls=%fused_computation.100 | convolution fusion | flops 17181966336 | bytes 29360128 | tf_op jit(solution)/shard_map/rf,df->rd/dot_general | solution.py:179
  528.6 62.3 %all-to-all-done.1 = bf16[8,256,1024]{2,1,0:T(8,128)(2,1)} async-done(((bf16[8,256,1024]{2,1,0:T(8,128)(2,1)}), bf16[8,256,1024]{2,1,0:T(8,128)(2,1)}, u32[]{:S(2)}, u32[]{:S(2)}) %all-to-all-start.1) | async-done | bytes 4194336 | tf_op jit(solution)/shard_map/all_to_all | solution.py:165
  612.6 75.3 %all-to-all-done.3 = bf16[8,256,1024]{2,1,0:T(8,128)(2,1)} async-done(((bf16[8,256,1024]{2,1,0:T(8,128)(2,1)}), bf16[8,256,1024]{2,1,0:T(8,128)(2,1)}, u32[]{:S(2)}, u32[]{:S(2)}) %all-to-all-start.3) | async-done | bytes 4194336 | tf_op jit(solution)/shard_map/all_to_all | solution.py:182
  728.5 227.9 %while.28 = (s32[]{:T(128)}, f32[1024,16,64]{0,2,1:T(8,128)}, f32[1024,16,64]{0,2,1:T(8,128)}, bf16[2,512,16,64]{1,3,2,0:T(8,128)(2,1)}, bf16[2,512,16,64]{1,3,2...) while((s32[]{:T(128)}, f32[1024,16,64]{0,2,1:T(8,128)}, ...), condition=%wide.region_17.18_spmd.clone, body=%wide.region_15.17_spmd.clone.sunk | while | flops 5500822016 | bytes 325292288 | solution.py:107
  730.3 19.0 %fusion.155 = f32[16,512,1024]{2,1,0:T(8,128)} fusion(bf16[1024,16,64]{0,2,1:T(8,128)(2,1)} %get-tuple-element.422, bf16[2,512,16,64]{1,3,2,0:T(8,128)(2,1)} %get-tuple-element.420, s32[]{:T(128)S(6)} %copy.68), kind=kOutput, calls=%fused_computation.36.clone.1 | convolution fusion | flops 1073741824 | bytes 36700164 | tf_op jit(solution)/shard_map/while/body/eval_jaxpr/qhd,khd->hqk/dot_general | solution.py:38
  749.4 17.7 %bitcast_add_fusion.5 = f32[1024,16,64]{0,2,1:T(8,128)} fusion(f32[1024,16,64]{0,2,1:T(8,128)} %get-tuple-element.405, f32[16,512,1024]{2,1,0:T(8,128)} %fusion.155, f32[16,512]{1,0:T(8,128)S(1)} %dynamic-slice_bitcast_fusion.2, pred[512,1024]{1,0:T(8,128)(4,1)S(1)} %iota_compare_fusion.7, pred[]{:T(512)S(6)} %compare.3, ...), kind=kOutput, calls=%fused_computation.28.clone.1 | convolution fusion | flops 1109393408 | bytes 43548676 | tf_op jit(solution)/shard_map/while/body/eval_jaxpr/hqk,qhd->khd/dot_general | solution.py:81
  767.1 26.0 %multiply_reduce_fusion.4 = (f32[16,512]{1,0:T(8,128)S(1)}, f32[16,512,1024]{2,1,0:T(8,128)}) fusion(f32[16,512,1024]{2,1,0:T(8,128)} %fusion.155, f32[16,512]{1,0:T(8,128)S(1)} %dynamic-slice_bitcast_fusion.2, pred[512,1024]{1,0:T(8,128)(4,1)S(1)} %iota_compare_fusion.7, bf16[1024,16,64]{0,2,1:T(8,128)(2,1)} %get-tuple-element.425, ...), kind=kOutput, calls=%fused_computation.23.clone.1 | convolution fusion | flops 1115676672 | bytes 70844416 | tf_op jit(solution)/shard_map/while/body/eval_jaxpr/qhd,khd->hqk/dot_general | solution.py:87
  793.1 27.8 %multiply_convert_fusion.6 = bf16[16,512,1024]{2,1,0:T(8,128)(2,1)} fusion(f32[16,512,1024]{2,1,0:T(8,128)} %get-tuple-element.361, f32[16,512,1024]{2,1,0:T(8,128)} %fusion.155, f32[16,512]{1,0:T(8,128)S(1)} %get-tuple-element.362, f32[16,512]{1,0:T(8,128)S(1)} %dynamic-slice_bitcast_fusion.2, pred[512,1024]{1,0:T(8,128)(4,1)S(1)} %iota_compare_fusion.7), kind=kLoop, calls=%fused_computation.22.clone.1 | loop fusion | flops 50331648 | bytes 84475904 | tf_op jit(solution)/shard_map/while/body/eval_jaxpr/convert_element_type | solution.py:91
  844.3 17.5 %fusion.155 = f32[16,512,1024]{2,1,0:T(8,128)} fusion(bf16[1024,16,64]{0,2,1:T(8,128)(2,1)} %get-tuple-element.422, bf16[2,512,16,64]{1,3,2,0:T(8,128)(2,1)} %get-tuple-element.420, s32[]{:T(128)S(6)} %copy.68), kind=kOutput, calls=%fused_computation.36.clone.1 | convolution fusion | flops 1073741824 | bytes 36700164 | tf_op jit(solution)/shard_map/while/body/eval_jaxpr/qhd,khd->hqk/dot_general | solution.py:38
  861.9 18.7 %bitcast_add_fusion.5 = f32[1024,16,64]{0,2,1:T(8,128)} fusion(f32[1024,16,64]{0,2,1:T(8,128)} %get-tuple-element.405, f32[16,512,1024]{2,1,0:T(8,128)} %fusion.155, f32[16,512]{1,0:T(8,128)S(1)} %dynamic-slice_bitcast_fusion.2, pred[512,1024]{1,0:T(8,128)(4,1)S(1)} %iota_compare_fusion.7, pred[]{:T(512)S(6)} %compare.3, ...), kind=kOutput, calls=%fused_computation.28.clone.1 | convolution fusion | flops 1109393408 | bytes 43548676 | tf_op jit(solution)/shard_map/while/body/eval_jaxpr/hqk,qhd->khd/dot_general | solution.py:81
  880.6 25.9 %multiply_reduce_fusion.4 = (f32[16,512]{1,0:T(8,128)S(1)}, f32[16,512,1024]{2,1,0:T(8,128)}) fusion(f32[16,512,1024]{2,1,0:T(8,128)} %fusion.155, f32[16,512]{1,0:T(8,128)S(1)} %dynamic-slice_bitcast_fusion.2, pred[512,1024]{1,0:T(8,128)(4,1)S(1)} %iota_compare_fusion.7, bf16[1024,16,64]{0,2,1:T(8,128)(2,1)} %get-tuple-element.425, ...), kind=kOutput, calls=%fused_computation.23.clone.1 | convolution fusion | flops 1115676672 | bytes 70844416 | tf_op jit(solution)/shard_map/while/body/eval_jaxpr/qhd,khd->hqk/dot_general | solution.py:87
  906.5 27.8 %multiply_convert_fusion.6 = bf16[16,512,1024]{2,1,0:T(8,128)(2,1)} fusion(f32[16,512,1024]{2,1,0:T(8,128)} %get-tuple-element.361, f32[16,512,1024]{2,1,0:T(8,128)} %fusion.155, f32[16,512]{1,0:T(8,128)S(1)} %get-tuple-element.362, f32[16,512]{1,0:T(8,128)S(1)} %dynamic-slice_bitcast_fusion.2, pred[512,1024]{1,0:T(8,128)(4,1)S(1)} %iota_compare_fusion.7), kind=kLoop, calls=%fused_computation.22.clone.1 | loop fusion | flops 50331648 | bytes 84475904 | tf_op jit(solution)/shard_map/while/body/eval_jaxpr/convert_element_type | solution.py:91
  1007.1 39.1 %all-reduce = (f32[1024]{0:T(1024)}, f32[1024]{0:T(1024)}) all-reduce(f32[1024]{0:T(1024)S(1)} %get-tuple-element.196, f32[1024]{0:T(1024)S(1)} %copy-done.41), channel_id=1, replica_groups=mesh['expert'=8,'replica'=4] {'expert','replica'}, use_global_device_ids=true, to_apply=%region_21.22 | all-reduce | flops 2048 | bytes 16384 | tf_op jit(solution)/shard_map/psum | solution.py:245
  1070.0 193.1 %all-reduce.4.cloned.1.call-done = (f32[1024,1024]{1,0:T(8,128)}, f32[1024,1024]{1,0:T(8,128)}, f32[1024,1024]{1,0:T(8,128)}, f32[1024,1024]{1,0:T(8,128)}) async-done(((f32[1024,1024]{1,0:T(8,128)}, f32[1024,1024]{1,0:T(8,128)}, f32[1024,1024]{1,0:T(8,128)}, f32[1024,1024]{1,0:T(8,128)}), (f32[1024,1024]{1,0:T(8,128)}, f32[1024,1024]{1,0:T(8,128)}, f32[1024,1024]{1,0:T(8,128)}, ...) | async-done | bytes 16777232 | tf_op jit(solution)/shard_map/psum | solution.py:245
  (223 shorter events, 353.6 us)
Async XLA Ops:
  8.0 13.9 %copy-start = (bf16[1024,1024]{1,0:T(8,128)(2,1)S(1)}, bf16[1024,1024]{1,0:T(8,128)(2,1)}, u32[]{:S(2)}) copy-start(bf16[1024,1024]{1,0:T(8,128)(2,1)} %param.20) | copy-start | bytes 6291460
  13.7 8.3 copy-start.43
  19.7 10.3 copy-start.35
  22.0 8.1 copy-start.39
  63.6 15.3 %copy-start.5 = (bf16[1024,16,64]{0,2,1:T(8,128)(2,1)S(1)}, bf16[1024,16,64]{0,2,1:T(8,128)(2,1)}, u32[]{:S(2)}) copy-start(bf16[1024,16,64]{0,2,1:T(8,128)(2,1)} %get-tuple-element.387) | copy-start | bytes 6291460 | tf_op jit(solution)/shard_map/while
  63.6 15.3 %copy-start.25 = (bf16[2,512,16,64]{1,3,2,0:T(8,128)(2,1)S(1)}, bf16[2,512,16,64]{1,3,2,0:T(8,128)(2,1)}, u32[]{:S(2)}) copy-start(bf16[2,512,16,64]{1,3,2,0:T(8,128)(2,1)} %get-tuple-element.373) | copy-start | bytes 6291460 | tf_op jit(solution)/shard_map/while
  112.2 15.3 %copy-start.5 = (bf16[1024,16,64]{0,2,1:T(8,128)(2,1)S(1)}, bf16[1024,16,64]{0,2,1:T(8,128)(2,1)}, u32[]{:S(2)}) copy-start(bf16[1024,16,64]{0,2,1:T(8,128)(2,1)} %get-tuple-element.387) | copy-start | bytes 6291460 | tf_op jit(solution)/shard_map/while
  112.2 15.3 %copy-start.25 = (bf16[2,512,16,64]{1,3,2,0:T(8,128)(2,1)S(1)}, bf16[2,512,16,64]{1,3,2,0:T(8,128)(2,1)}, u32[]{:S(2)}) copy-start(bf16[2,512,16,64]{1,3,2,0:T(8,128)(2,1)} %get-tuple-element.373) | copy-start | bytes 6291460 | tf_op jit(solution)/shard_map/while
  167.7 100.8 %all-to-all-start = ((bf16[8,256,1024]{2,1,0:T(8,128)(2,1)}), bf16[8,256,1024]{2,1,0:T(8,128)(2,1)}, u32[]{:S(2)}, u32[]{:S(2)}) async-start(bf16[8,256,1024]{2,1,0:T(8,128)(2,1)} %bitcast.170), calls=%async_computation | async-start | bytes 8388608 | tf_op jit(solution)/shard_map/all_to_all | solution.py:156
  268.5 97.1 %all-to-all-start.2 = ((bf16[8,256,1024]{2,1,0:T(8,128)(2,1)}), bf16[8,256,1024]{2,1,0:T(8,128)(2,1)}, u32[]{:S(2)}, u32[]{:S(2)}) async-start(bf16[8,256,1024]{2,1,0:T(8,128)(2,1)} %bitcast.169), calls=%async_computation.2 | async-start | bytes 8388608 | tf_op jit(solution)/shard_map/all_to_all | solution.py:171
  273.1 231.7 %reduce-scatter.3.cloned.1.call-start = ((), (), s32[]{:S(2)}) async-start(), calls=%async_computation.6 | async-start | bytes 10485760 | tf_op jit(solution)/shard_map/reduce_scatter | solution.py:192
  433.9 294.5 %reduce-scatter.5.cloned.1.call-start = ((), (), s32[]{:S(2)}) async-start(), calls=%async_computation.8 | async-start | bytes 10485760 | tf_op jit(solution)/shard_map/reduce_scatter | solution.py:195
  494.4 96.4 %all-to-all-start.1 = ((bf16[8,256,1024]{2,1,0:T(8,128)(2,1)}), bf16[8,256,1024]{2,1,0:T(8,128)(2,1)}, u32[]{:S(2)}, u32[]{:S(2)}) async-start(bf16[8,256,1024]{2,1,0:T(8,128)(2,1)} %bitcast.174), calls=%async_computation.1 | async-start | bytes 8388608 | tf_op jit(solution)/shard_map/all_to_all | solution.py:165
  499.0 547.1 %all-gather.3.cloned.1.call-start = ((), (), s32[]{:S(2)}) async-start(), calls=%async_computation.7 | async-start | bytes 10485760 | tf_op jit(solution)/shard_map/all_gather | solution.py:200
  590.9 97.1 %all-to-all-start.3 = ((bf16[8,256,1024]{2,1,0:T(8,128)(2,1)}), bf16[8,256,1024]{2,1,0:T(8,128)(2,1)}, u32[]{:S(2)}, u32[]{:S(2)}) async-start(bf16[8,256,1024]{2,1,0:T(8,128)(2,1)} %bitcast.173), calls=%async_computation.3 | async-start | bytes 8388608 | tf_op jit(solution)/shard_map/all_to_all | solution.py:182
  595.5 462.8 %all-gather.5.cloned.1.call-start = ((), (), s32[]{:S(2)}) async-start(), calls=%async_computation.9 | async-start | bytes 10485760 | tf_op jit(solution)/shard_map/all_gather | solution.py:203
  705.9 7.0 copy-start.46
  728.5 534.6 %all-reduce.4.cloned.1.call-start = ((), (), s32[]{:S(2)}) async-start(), calls=%async_computation.10 | async-start | bytes 33554432 | tf_op jit(solution)/shard_map/psum | solution.py:245
  820.9 10.4 copy-start.1
  820.9 10.4 copy-start.4
  934.3 10.3 copy-start.1
  934.3 10.3 copy-start.4
  960.9 13.2 %copy-start.27 = (bf16[128,8,2,512]{3,1,2,0:T(8,128)(2,1)}, bf16[128,8,2,512]{3,1,2,0:T(8,128)(2,1)S(1)}, u32[]{:S(2)}) copy-start(bf16[128,8,2,512]{3,1,2,0:T(8,128)(2,1)S(1)} %copy.50) | copy-start | bytes 6291460
  961.3 8.4 copy-start.22
  (41 other events, 151.7 us)
Sparse Core Ops, SparseCore 0:
  434.1 70.7 reduce-scatter.2
  507.6 71.7 reduce-scatter.4
  580.9 58.2 all-gather.2
  728.6 57.3 all-gather.4
Sparse Core Ops, SparseCore 1:
  983.0 280.0 all-reduce.3
where the time goes:
time: 1290 us; the launch traced here: 1280 us
  waiting for transfers between devices  489 us (38%)
  matrix products  449 us (35%)
  other arithmetic  138 us (11%)
  local copies, waits for them, and re-layouts  129 us (10%)
  blocking collectives  39.1 us (3%)
  starting transfers between devices  21.5 us (2%)
  between operations  16 us (1%)
    psum x1, waiting for transfers between devices, per_device(): lax.psum((grad_query_weight, grad_key_weight, grad_value_weight, grad_out...  193 us
    all_to_all x1, waiting for transfers between devices, per_device(): lax.all_to_all(outgoing.reshape(slab_shape), 'expert', split_axis=0, conc...  84.6 us
    all_to_all x1, waiting for transfers between devices, per_device(): lax.all_to_all(grad_rows.reshape(slab_shape), 'expert', split_axis=0, con...  75.3 us
    dot_general x6, matrix products, project(): return jnp.dot(left, right, preferred_element_type=jnp.float32)  68.4 us
    dot_general x4, matrix products, causal_scores(): jnp.einsum('qhd,khd->hqk', query_rows, key_heads, preferred_element_type=...  67.8 us
    all_to_all x1, waiting for transfers between devices, per_device(): lax.all_to_all(grad_outgoing.reshape(slab_shape), 'expert', split_axis=0,...  67.5 us
    all_to_all x1, waiting for transfers between devices, per_device(): lax.all_to_all(expert_result.reshape(slab_shape), 'expert', split_axis=0,...  62.3 us
    convert_element_type x2, other arithmetic, one_block(): grad_scores = grad_scores.astype(jnp.bfloat16)  55.6 us
  transfers between devices with their start and end apart: 9, of which 6 were waited for; matrix products, arithmetic and copies ran while one was open for 36% of the time, Pallas kernels for 0%

commit v1 on v0

v1 whole, which is shorter than its diff:
```python
import functools
import math

import jax
import jax.numpy as jnp
from jax import lax
from jax.experimental import pallas as pl
from jax.experimental.pallas import tpu as pltpu
from jax.sharding import PartitionSpec as P

HEAD_DIM=64
F32=jnp.float32; BF=jnp.bfloat16
MESH=pl.DeviceIdType.MESH
epsilon=1e-5
def dot(a,b): return jnp.dot(a,b,preferred_element_type=F32)
def dg(a,b,ca,cb): return lax.dot_general(a,b,(((ca,),(cb,)),((),())),preferred_element_type=F32)

def xor(a,b,count):
    total=0; step=1
    while step<count:
        x=(a//step)%2; y=(b//step)%2
        total=total+step*(x+y-2*x*y); step*=2
    return total

def norm_stats(rows):
    average=jnp.mean(rows,axis=-1,keepdims=True)
    centred=rows-average
    inverse=lax.rsqrt(jnp.mean(centred*centred,axis=-1,keepdims=True)+epsilon)
    return centred*inverse,inverse

def fwd_head(qT,kT,vT,block):
    seq=qT.shape[1]
    qs=qT*jnp.asarray(HEAD_DIM**-0.5,BF)
    k=kT.T
    outs=[]; lses=[]
    for i in range(seq//block):
        b=i*block; n=b+block
        diag=dot(k[b:n],qs[:,b:n])
        rows=lax.broadcasted_iota(jnp.int32,(block,block),0); cols=lax.broadcasted_iota(jnp.int32,(block,block),1)
        diag=jnp.where(rows<=cols,diag,-1e30)
        m=jnp.max(diag,axis=0,keepdims=True)
        if i:
            s=dot(k[:b],qs[:,b:n])
            m=jnp.maximum(m,jnp.max(s,axis=0,keepdims=True))
        p=jnp.exp(diag-m)
        l=jnp.sum(p,axis=0,keepdims=True)
        o=dot(vT[:,b:n],p.astype(BF))
        if i:
            p=jnp.exp(s-m)
            l=l+jnp.sum(p,axis=0,keepdims=True)
            o=o+dot(vT[:,:b],p.astype(BF))
        outs.append((o*(1.0/l)).astype(BF)); lses.append(m+jnp.log(l))
    return outs,lses

def onehot_rows(slot,first,count):
    ids=(lax.broadcasted_iota(jnp.int32,(count,slot.shape[1]),0)+first).astype(F32)
    return jnp.where(ids==slot,1.0,0.0).astype(BF)

def front_kernel(groups,cap,block,tok,rt,cot,g1,g2,wq,wk,wv,wo,
                 normed,q,k,v,att,lse,hid,pack,slot,cotarr,
                 cpack,n2,ssem,rsem,lsem):
    T,D=tok.shape
    R=256
    me=lax.axis_index("expert")
    barrier=pltpu.get_barrier_semaphore()
    def greet(i,c):
        pl.semaphore_signal(barrier,inc=1,device_id={"expert":xor(me,i,groups)},device_id_type=MESH)
        return c
    lax.fori_loop(1,groups,greet,0)
    routes=rt[...]
    e=jnp.where(lax.broadcasted_iota(jnp.int32,(groups,T),0)==routes,1.0,0.0)
    tri=jnp.where(lax.broadcasted_iota(jnp.int32,(T,T),0)<=lax.broadcasted_iota(jnp.int32,(T,T),1),1.0,0.0).astype(BF)
    cum=dot(e.astype(BF),tri)
    rank=jnp.sum(cum*e,axis=0,keepdims=True)-1.0
    slots=routes.astype(F32)*cap+rank
    slot[...]=slots
    pl.semaphore_wait(barrier,groups-1)
    def push(i,c):
        peer=xor(me,groups-1-i,groups)
        cpack[peer]=dot(onehot_rows(slots,peer*cap,cap),cot[...]).astype(BF)
        pltpu.make_async_remote_copy(src_ref=cpack.at[peer],dst_ref=cotarr.at[me],send_sem=ssem.at[peer],recv_sem=rsem.at[me],
            device_id={"expert":peer},device_id_type=MESH).start()
        return c
    lax.fori_loop(0,groups-1,push,0)
    cpack[me]=dot(onehot_rows(slots,me*cap,cap),cot[...]).astype(BF)
    own=pltpu.make_async_copy(cpack.at[me],cotarr.at[me],lsem)
    own.start()
    def norm_one(i,c):
        r=pl.ds(pl.multiple_of(i*R,R),R)
        u,_=norm_stats(tok[r,:].astype(F32))
        normed[r,:]=(u*g1[...]).astype(BF)
        return c
    lax.fori_loop(0,T//R,norm_one,0)
    def proj(i,c):
        s=pl.ds(pl.multiple_of(i*R,R),R)
        for w,o in ((wq,q),(wk,k),(wv,v)):
            o[s,:]=dg(w[:,s],normed[...],0,1).astype(BF)
        return c
    lax.fori_loop(0,D//R,proj,0)
    def head(h,c):
        s=pl.ds(pl.multiple_of(h*HEAD_DIM,HEAD_DIM),HEAD_DIM)
        outs,lses=fwd_head(q[s,:],k[s,:],v[s,:],block)
        att[s,:]=jnp.concatenate(outs,axis=1)
        lse[pl.ds(h,1),:]=jnp.concatenate(lses,axis=1)
        return c
    lax.fori_loop(0,D//HEAD_DIM,head,0)
    def out(i,c):
        r=pl.ds(pl.multiple_of(i*R,R),R)
        h=tok[r,:].astype(F32)+dg(att[:,r],wo[...],0,0)
        hid[r,:]=h
        u,_=norm_stats(h)
        n2[r,:]=(u*g2[...]).astype(BF)
        return c
    lax.fori_loop(0,T//R,out,0)
    def packing(i,c):
        pack[i]=dot(onehot_rows(slots,i*cap,cap),n2[...]).astype(BF)
        return c
    lax.fori_loop(0,groups,packing,0)
    own.wait()
    def finish(i,c):
        peer=xor(me,i,groups)
        pltpu.make_async_remote_copy(src_ref=cpack.at[peer],dst_ref=cotarr.at[peer],send_sem=ssem.at[peer],recv_sem=rsem.at[peer],
            device_id={"expert":peer},device_id_type=MESH).wait()
        return c
    lax.fori_loop(1,groups,finish,0)

def front(tokens,routes_row,cot,g1,g2,wq,wk,wv,wo,groups,cap,block=512):
    T,D=tokens.shape
    H=D//HEAD_DIM
    V=pl.BlockSpec(memory_space=pltpu.VMEM)
    A=pl.BlockSpec(memory_space=pl.ANY)
    sd=jax.ShapeDtypeStruct
    return pl.pallas_call(functools.partial(front_kernel,groups,cap,block),
      in_specs=[V]*9,out_specs=[V]*9+[A],
      out_shape=[sd((T,D),BF)]+[sd((D,T),BF)]*4+[sd((H,T),F32),sd((T,D),F32),sd((groups,cap,D),BF),sd((1,T),F32),sd((groups,cap,D),BF)],
      scratch_shapes=[pltpu.VMEM((groups,cap,D),BF),pltpu.VMEM((T,D),BF),pltpu.SemaphoreType.DMA((groups,)),pltpu.SemaphoreType.DMA((groups,)),pltpu.SemaphoreType.DMA],
      compiler_params=pltpu.CompilerParams(vmem_limit_bytes=60*2**20,collective_id=0,has_side_effects=True),
      name="front")(tokens,routes_row,cot,g1,g2,wq,wk,wv,wo)


F32=jnp.float32; BF=jnp.bfloat16
MESH=pl.DeviceIdType.MESH
def dot(a,b): return jnp.dot(a,b,preferred_element_type=F32)
def dg(a,b,ca,cb): return lax.dot_general(a,b,(((ca,),(cb,)),((),())),preferred_element_type=F32)
def xor(a,b,count):
    total=0; step=1
    while step<count:
        x=(a//step)%2; y=(b//step)%2
        total=total+step*(x+y-2*x*y); step*=2
    return total
SQ=math.sqrt(2/math.pi)
def gelu_pair(h):
    h2=h*h
    th=jnp.tanh(h*(SQ+SQ*0.044715*h2))
    half=0.5*(1.0+th)
    act=h*half
    slope=half+act*((1.0-th)*(SQ+3*SQ*0.044715*h2))
    return act,slope

def expert_kernel(groups,cap,pack,cotarr,up,down,gback,ret,dup,ddown,act,
                  arr,upv,downv,cotv,gpre,actb,gst,retb,stage,
                  psend,precv,gsend,grecv,wsem,retsem,actsem,stsem,tsem):
    rows=groups*cap
    D,F=upv.shape
    FT=1024
    me=lax.axis_index("expert")
    barrier=pltpu.get_barrier_semaphore()
    def greet(i,c):
        pl.semaphore_signal(barrier,inc=1,device_id={"expert":xor(me,i,groups)},device_id_type=MESH)
        return c
    lax.fori_loop(1,groups,greet,0)
    pl.semaphore_wait(barrier,groups-1)
    def at(j): return pl.ds(pl.multiple_of(j*cap,cap),cap)
    def dispatch(j,i):
        return pltpu.make_async_remote_copy(src_ref=pack.at[j],dst_ref=arr.at[at(me)],send_sem=psend.at[i],recv_sem=precv.at[i],
            device_id={"expert":j},device_id_type=MESH)
    def giveback(j,i):
        return pltpu.make_async_remote_copy(src_ref=gst.at[at(j)],dst_ref=gback.at[me],send_sem=gsend.at[i],recv_sem=grecv.at[i],
            device_id={"expert":j},device_id_type=MESH)
    half=groups//2
    def push(i,c):
        dispatch(xor(me,i,groups),i).start()
        return c
    lax.fori_loop(half,half+half//2,push,0)
    lax.fori_loop(1,half,push,0)
    own=pltpu.make_async_copy(pack.at[me],arr.at[at(me)],precv.at[0])
    own.start()
    cup=pltpu.make_async_copy(up,upv,wsem.at[0]); cup.start()
    ccot=pltpu.make_async_copy(cotarr,cotv,wsem.at[1]); ccot.start()
    cdown=pltpu.make_async_copy(down,downv,wsem.at[2]); cdown.start()
    cup.wait(); ccot.wait(); cdown.wait()
    def retcopy(j,b): return pltpu.make_async_copy(retb.at[b],ret.at[j],retsem.at[b])
    def actcopy(j,b): return pltpu.make_async_copy(actb.at[b],act.at[at(j)],actsem.at[b])
    def chunk(i,c):
        j=xor(me,i,groups)
        b=i%2
        @pl.when(i==0)
        def _(): own.wait()
        @pl.when(i>0)
        def _(): dispatch(j,i).wait_recv()
        @pl.when(i==half-1)
        def _(): lax.fori_loop(half+half//2,groups,push,0)
        @pl.when(i>=2)
        def _():
            retcopy(j,b).wait(); actcopy(j,b).wait()
        def tile(t,c):
            s=pl.ds(pl.multiple_of(t*FT,FT),FT)
            h=dot(arr[at(j),:],upv[:,s])
            g=dg(cotv[j],downv[s,:],1,1)
            a,slope=gelu_pair(h)
            actb[b,:,s]=a.astype(BF)
            gpre[at(j),s]=(g*slope).astype(BF)
            return c
        lax.fori_loop(0,F//FT,tile,0)
        gst[at(j),:]=dg(gpre[at(j),:],upv[...],1,1).astype(BF)
        @pl.when(i>0)
        def _(): giveback(j,i).start()
        @pl.when(i==0)
        def _(): pltpu.make_async_copy(gst.at[at(j)],gback.at[me],grecv.at[0]).start()
        actcopy(j,b).start()
        retb[b]=dot(actb[b],downv[...]).astype(BF)
        retcopy(j,b).start()
        return c
    lax.fori_loop(0,groups,chunk,0)
    for b in range(2):
        retcopy(0,b).wait(); actcopy(0,b).wait()
    def atile(t,b): return pltpu.make_async_copy(act.at[:,pl.ds(pl.multiple_of(t*D,D),D)],downv.at[pl.ds(b*rows,rows)],tsem.at[b])
    atile(0,0).start(); atile(1,1).start()
    S=512
    def upout(t,b): return pltpu.make_async_copy(stage.at[b],dup.at[:,pl.ds(pl.multiple_of(t*S,S),S)],stsem.at[b])
    def dup_tile(t,c):
        b=t%2
        @pl.when(t>=2)
        def _(): upout(t,b).wait()
        def part(k,c):
            r=pl.ds(pl.multiple_of(k*S,S),S)
            stage[b,r,:]=dg(arr[:,r],gpre[:,pl.ds(pl.multiple_of(t*S,S),S)],0,0).astype(BF)
            return c
        lax.fori_loop(0,D//S,part,0)
        upout(t,b).start()
        return c
    lax.fori_loop(0,F//S,dup_tile,0)
    for b in range(2): upout(b,b).wait()
    def downout(f,b): return pltpu.make_async_copy(upv.at[pl.ds(b*S,S),pl.ds(0,D)],ddown.at[pl.ds(pl.multiple_of(f*S,S),S)],stsem.at[b])
    def ddown_tile(t,c):
        tb=t%2
        atile(t,tb).wait()
        def part(p,c):
            b=p%2
            @pl.when(t*(D//S)+p>=2)
            def _(): downout(0,b).wait()
            a=downv[pl.ds(pl.multiple_of(tb*rows,rows),rows),pl.ds(pl.multiple_of(p*S,S),S)]
            upv[pl.ds(pl.multiple_of(b*S,S),S),pl.ds(0,D)]=dg(a,cotv[...].reshape(rows,D),0,0).astype(BF)
            downout(t*(D//S)+p,b).start()
            return c
        lax.fori_loop(0,D//S,part,0)
        @pl.when(t+2<F//D)
        def _(): atile(t+2,tb).start()
        return c
    lax.fori_loop(0,F//D,ddown_tile,0)
    for b in range(2): downout(b,b).wait()
    pltpu.make_async_copy(gst.at[at(me)],gback.at[me],grecv.at[0]).wait()
    def finish(i,c):
        j=xor(me,i,groups)
        dispatch(j,i).wait_send()
        giveback(j,i).wait()
        return c
    lax.fori_loop(1,groups,finish,0)

def expert(pack,cotarr,up,down):
    groups,cap,D=pack.shape
    F=up.shape[1]; rows=groups*cap
    A=pl.BlockSpec(memory_space=pl.ANY)
    sd=jax.ShapeDtypeStruct
    DMA=pltpu.SemaphoreType.DMA
    return pl.pallas_call(functools.partial(expert_kernel,groups,cap),
      in_specs=[A]*4,out_specs=[A]*5,
      out_shape=[sd((groups,cap,D),BF)]*2+[sd((D,F),BF),sd((F,D),BF),sd((rows,F),BF)],
      scratch_shapes=[pltpu.VMEM((rows,D),BF),pltpu.VMEM((D,F),BF),pltpu.VMEM((F,D),BF),pltpu.VMEM((groups,cap,D),BF),pltpu.VMEM((rows,F),BF),
         pltpu.VMEM((2,cap,F),BF),pltpu.VMEM((rows,D),BF),pltpu.VMEM((2,cap,D),BF),pltpu.VMEM((2,D,512),BF),
         DMA((groups,)),DMA((groups,)),DMA((groups,)),DMA((groups,)),DMA((3,)),DMA((2,)),DMA((2,)),DMA((2,)),DMA((2,))],
      compiler_params=pltpu.CompilerParams(vmem_limit_bytes=63*2**20,collective_id=1,has_side_effects=True),
      name="experts")(pack,cotarr,up,down)


def bwd_head(qT,kT,vT,oT,doT,lse,block):
    seq=qT.shape[1]
    scale=HEAD_DIM**-0.5
    qs=qT*jnp.asarray(scale,BF)
    q=qs.T; k=kT.T; v=vT.T; do=doT.T
    delta=jnp.sum(oT.astype(F32)*doT.astype(F32),axis=0,keepdims=True)
    count=seq//block
    dqs=[None]*count; dks=[]; dvs=[]
    for j in range(count):
        b=j*block
        kj=k[b:b+block]; vj=v[b:b+block]
        s=dot(kj,qs[:,b:])
        n=seq-b
        rows=lax.broadcasted_iota(jnp.int32,(block,n),0); cols=lax.broadcasted_iota(jnp.int32,(block,n),1)
        p=jnp.where(rows<=cols,jnp.exp(s-lse[:,b:]),0.0)
        dp=dot(vj,doT[:,b:])
        ds=(p*(dp-delta[:,b:])).astype(BF)
        dvs.append(dot(p.astype(BF),do[b:]))
        dks.append(dot(ds,q[b:]))
        c=dot(kT[:,b:b+block],ds)
        for i in range(j,count):
            part=c[:,(i-j)*block:(i-j+1)*block]
            dqs[i]=part if dqs[i] is None else dqs[i]+part
    return [(x*scale).astype(BF).T for x in dqs],[x.astype(BF) for x in dks],[x.astype(BF) for x in dvs]

def back_kernel(groups,cap,block,
        gback,ret,slot,hid,cot,tok,normed,q,k,v,att,lse,g1,g2,wq,wk,wv,wo,
        output,gtok,dw,dgain,rarr,
        vslots,vhid,vcot,vtok,vnormed,vq,vk,vv,vatt,vwq,vwk,vwv,vwo,ghl,datt,dq,dk,dv,
        isem,ssem,rsem,lsem):
    T,D=vtok.shape
    R=256
    rows=groups*cap
    me=lax.axis_index("expert")
    barrier=pltpu.get_barrier_semaphore()
    def greet(i,c):
        pl.semaphore_signal(barrier,inc=1,device_id={"expert":xor(me,i,groups)},device_id_type=MESH)
        return c
    lax.fori_loop(1,groups,greet,0)
    copies=[pltpu.make_async_copy(a,b,isem.at[i]) for i,(a,b) in enumerate(
        ((gback,vslots),(hid,vhid),(cot,vcot),(wo,vwo),(att,vatt),(q,vq),(k,vk),(v,vv),(normed,vnormed),(wq,vwq),(wk,vwk),(wv,vwv),(tok,vtok)))]
    for c in copies: c.start()
    pl.semaphore_wait(barrier,groups-1)
    def send(i):
        j=xor(me,i,groups)
        return pltpu.make_async_remote_copy(src_ref=ret.at[j],dst_ref=rarr.at[me],send_sem=ssem.at[i],recv_sem=rsem.at[i],
            device_id={"expert":j},device_id_type=MESH)
    def push(i,c):
        send(groups-i).start()
        return c
    lax.fori_loop(1,groups,push,0)
    own=pltpu.make_async_copy(ret.at[me],rarr.at[me],lsem); own.start()
    def gathered(r):
        col=jnp.broadcast_to(slot[:,r],(128,R)).T[:,:1]
        ids=lax.broadcasted_iota(jnp.int32,(R,rows),1).astype(F32)
        return dot(jnp.where(ids==col,1.0,0.0).astype(BF),vslots[...].reshape(rows,D))
    for c in copies[:3]: c.wait()
    dgain[...]=jnp.zeros_like(dgain)
    def norm_two(i,c):
        r=pl.ds(pl.multiple_of(i*R,R),R)
        gs=gathered(r)
        u,inv=norm_stats(vhid[r,:])
        m=gs*g2[...]
        dgain[1:2,:]+=jnp.sum(gs*u,axis=0,keepdims=True)
        gh=vcot[r,:].astype(F32)+inv*(m-jnp.mean(m,axis=-1,keepdims=True)-u*jnp.mean(m*u,axis=-1,keepdims=True))
        gtok[r,:]=gh
        ghl[r,:]=gh.astype(BF)
        return c
    lax.fori_loop(0,T//R,norm_two,0)
    for c in copies[3:5]: c.wait()
    def outproj(i,c):
        s=pl.ds(pl.multiple_of(i*R,R),R)
        datt[s,:]=dg(vwo[s,:],ghl[...],1,1).astype(BF)
        dw[3,s,:]=dot(vatt[s,:],ghl[...]).astype(BF)
        return c
    lax.fori_loop(0,D//R,outproj,0)
    for c in copies[5:]: c.wait()
    def pair(h,c):
        w=2*HEAD_DIM
        col=pl.ds(pl.multiple_of(h*w,w),w)
        res=[]
        for a in range(2):
            s=pl.ds(pl.multiple_of(h*w+a*HEAD_DIM,HEAD_DIM),HEAD_DIM)
            res.append(bwd_head(vq[s,:],vk[s,:],vv[s,:],vatt[s,:],datt[s,:],lse[pl.ds(2*h+a,1),:],block))
        for ref,x,y in zip((dq,dk,dv),*res):
            for i in range(T//block):
                ref[i*block:(i+1)*block,col]=jnp.concatenate([x[i],y[i]],axis=1)
        return c
    lax.fori_loop(0,D//(2*HEAD_DIM),pair,0)
    def wgrad(i,c):
        s=pl.ds(pl.multiple_of(i*R,R),R)
        for n,x in enumerate((dq,dk,dv)):
            dw[n,s,:]=dg(vnormed[:,s],x[...],0,0).astype(BF)
        return c
    lax.fori_loop(0,D//R,wgrad,0)
    def norm_one(i,c):
        r=pl.ds(pl.multiple_of(i*R,R),R)
        gn=dg(dq[r,:],vwq[...],1,1)+dg(dk[r,:],vwk[...],1,1)+dg(dv[r,:],vwv[...],1,1)
        u,inv=norm_stats(vtok[r,:].astype(F32))
        m=gn*g1[...]
        dgain[0:1,:]+=jnp.sum(gn*u,axis=0,keepdims=True)
        gtok[r,:]+=inv*(m-jnp.mean(m,axis=-1,keepdims=True)-u*jnp.mean(m*u,axis=-1,keepdims=True))
        return c
    lax.fori_loop(0,T//R,norm_one,0)
    own.wait()
    def finish(i,c):
        send(i).wait()
        return c
    lax.fori_loop(1,groups,finish,0)
    load=pltpu.make_async_copy(rarr,vslots,lsem); load.start(); load.wait()
    def final(i,c):
        r=pl.ds(pl.multiple_of(i*R,R),R)
        output[r,:]=(vhid[r,:]+gathered(r)).astype(BF)
        return c
    lax.fori_loop(0,T//R,final,0)

def back(gback,ret,slot,hid,cot,tok,normed,q,k,v,att,lse,g1,g2,wq,wk,wv,wo,block=256):
    groups,cap,D=ret.shape
    T=tok.shape[0]
    V=pl.BlockSpec(memory_space=pltpu.VMEM)
    A=pl.BlockSpec(memory_space=pl.ANY)
    sd=jax.ShapeDtypeStruct
    DMA=pltpu.SemaphoreType.DMA
    dn=(D,T)
    return pl.pallas_call(functools.partial(back_kernel,groups,cap,block),
      in_specs=[A,A,V]+[A]*8+[V]*3+[A]*4,out_specs=[V]*4+[A],
      out_shape=[sd((T,D),BF),sd((T,D),F32),sd((4,D,D),BF),sd((8,D),F32),sd((groups,cap,D),BF)],
      scratch_shapes=[pltpu.VMEM((groups,cap,D),BF),pltpu.VMEM((T,D),F32)]+[pltpu.VMEM((T,D),BF)]*3+[pltpu.VMEM((D,T),BF)]*4+[pltpu.VMEM((D,D),BF)]*4
         +[pltpu.VMEM((T,D),BF),pltpu.VMEM((D,T),BF)]+[pltpu.VMEM((T,D),BF)]*3+[DMA((13,)),DMA((groups,)),DMA((groups,)),DMA],
      compiler_params=pltpu.CompilerParams(vmem_limit_bytes=63*2**20,collective_id=2,has_side_effects=True),
      name="back")(gback,ret,slot,hid,cot,tok,normed,q,k,v,att,lse,g1,g2,wq,wk,wv,wo)


def per_device(tokens,routes,gain_one,query_weight,key_weight,value_weight,out_weight,gain_two,up_weight,down_weight,cotangent):
    T,D=tokens.shape
    groups=lax.axis_size("expert")
    cap=2*T//groups
    g1=gain_one.reshape(1,D); g2=gain_two.reshape(1,D)
    weights=(query_weight,key_weight,value_weight,out_weight)
    normed,q,k,v,att,lse,hid,pack,slot,cotarr=front(tokens,routes.reshape(1,T),cotangent,g1,g2,*weights,groups,cap)
    gback,ret,dup,ddown,_=expert(pack,cotarr,up_weight[0],down_weight[0])
    output,gtok,dw,dgain,_=back(gback,ret,slot,hid,cotangent,tokens,normed,q,k,v,att,lse,g1,g2,*weights)
    sdown=lax.psum_scatter(ddown[None],"replica",scatter_dimension=1,tiled=True)
    sup=lax.psum_scatter(dup[None],"replica",scatter_dimension=2,tiled=True)
    gdown=lax.all_gather(sdown,"replica",axis=1,tiled=True).astype(F32)
    gup=lax.all_gather(sup,"replica",axis=2,tiled=True).astype(F32)
    packed=jnp.concatenate([dw.reshape(4*D,D),dgain.astype(BF)],axis=0)
    total=lax.psum(packed,("expert","replica")).astype(F32)
    ws=[total[i*D:(i+1)*D] for i in range(4)]
    return (output,gtok,total[4*D],*ws,total[4*D+1],gup,gdown)


def solution(mesh):
    rows=P(("expert","replica"),None)
    each=P("expert",None,None)
    return jax.shard_map(per_device,mesh=mesh,
        in_specs=(rows,rows,P(),P(),P(),P(),P(),P(),each,each,rows),
        out_specs=(rows,rows,P(),P(),P(),P(),P(),P(),each,each),check_vma=False)
```

time: 1290 us -> 747 us (0.58)
  matrix products: 449 us -> 0 us
  Pallas kernels: 0 us -> 418 us
  waiting for transfers between devices: 489 us -> 265 us
  local copies, waits for them, and re-layouts: 129 us -> 16.5 us
  other arithmetic: 138 us -> 32.2 us
  blocking collectives: 39.1 us -> 0 us
  starting transfers between devices: 21.5 us -> 0.42 us
    dot_general x32 -> x0, matrix products: 449 us -> none  [the longest x6 68.4 us: project(): return jnp.dot(left, right, preferred_element_type=jnp.float32)]
    pallas_call x0 -> x3, Pallas kernels: none -> 418 us  [the longest x1 173 us: expert(): pl.pallas_call(functools.partial(expert_kernel, groups, cap), in_specs=[A...]
    all_to_all x4 -> x0, waiting for transfers between devices: 290 us -> none  [the longest x1 84.6 us: per_device(): lax.all_to_all(outgoing.reshape(slab_shape), 'expert', split_axis=0, conc...]
    convert_element_type x8 -> x3, other arithmetic: 82.8 us -> 24.4 us  [the longest x1 12 us: per_device(): gup = lax.all_gather(sup, 'replica', axis=2, tiled=True).astype(F32)]
    unnamed x99 -> x6, local copies, waits for them, and re-layouts: 46.7 us -> 4.96 us
    reduce_sum x7 -> x0, other arithmetic: 41.3 us -> none  [the longest x2 30.6 us: one_block(): summed = jnp.sum(exponent, axis=-1, keepdims=True)]
    psum x1 -> x0, blocking collectives: 39.1 us -> none  [per_device(): lax.psum((grad_query_weight, grad_key_weight, grad_value_weight, grad_out...]
    reduce_scatter x2, waiting for transfers between devices: 5.75 us -> 43.7 us  [the longest x1 43.7 us: per_device(): lax.psum_scatter(dup[None], 'replica', scatter_dimension=2, tiled=True)]
  transfers between devices with their start and end apart: 9 -> 5, of which waited for: 6 -> 2; matrix products, arithmetic and copies ran while one was open for 36% -> 4% of each run, Pallas kernels for 0% -> 17%
where the time goes in v1:
time: 747 us
  Pallas kernels  418 us (56%)
  waiting for transfers between devices  265 us (35%)
  other arithmetic  32.2 us (4%)
  local copies, waits for them, and re-layouts  16.5 us (2%)
  between operations  15.3 us (2%)
    psum x1, waiting for transfers between devices, per_device(): total = lax.psum(packed, ('expert', 'replica')).astype(F32)  220 us
    pallas_call x1, Pallas kernels, expert(): pl.pallas_call(functools.partial(expert_kernel, groups, cap), in_specs=[A...  173 us
    pallas_call x1, Pallas kernels, back(): pl.pallas_call(functools.partial(back_kernel, groups, cap, block), in_spe...  127 us
    pallas_call x1, Pallas kernels, front(): pl.pallas_call(functools.partial(front_kernel, groups, cap, block), in_sp...  118 us
    reduce_scatter x1, waiting for transfers between devices, per_device(): lax.psum_scatter(dup[None], 'replica', scatter_dimension=2, tiled=True)  43.7 us
  transfers between devices with their start and end apart: 5, of which 2 were waited for; matrix products, arithmetic and copies ran while one was open for 4% of the time, Pallas kernels for 17%

profile of v1, /device:TPU:0, one launch (start us, length us, event | category | flops | bytes accessed | tf_op | source)
XLA Modules:
  0.0 746.9 jit_solution(1016704902136911409)
XLA Ops:
  8.0 0.0 reduce-scatter.5.cloned.1.call-start
  8.1 117.5 %front.1 = (bf16[1024,1024]{1,0:T(8,128)(2,1)}, bf16[1024,1024]{1,0:T(8,128)(2,1)}, bf16[1024,1024]{1,0:T(8,128)(2,1)}, bf16[1024,1024]{1,0:T(8,128)(2,1)}, bf16...) custom-call(bf16[1024,1024]{1,0:T(8,128)(2,1)} %tok.3, ...), custom_call_target="tpu_custom_call" | custom-call | tf_op jit(solution)/shard_map/front/pallas_call | solution.py:133
  125.6 172.8 %experts.1 = (bf16[8,256,1024]{2,1,0:T(8,128)(2,1)}, bf16[8,256,1024]{2,1,0:T(8,128)(2,1)}, bf16[1024,4096]{1,0:T(8,128)(2,1)}, bf16[4096,1024]{1,0:T(8,128)(2,1)}, bf16[2048,4096]{1,0:T(8,128)(2,1)}) custom-call(bf16[8,256,1024]{2,1,0:T(8,128)(2,1)} %get-tuple-element.28.pack, bf16[8,256,1024]{2,1,0:T(8,128)(2,1)} %get-tuple-element.29.cotarr, ...), custom_call_target="tpu_custom_call" | custom-call | tf_op jit(solution)/shard_map/experts/pallas_call | solution.py:276
  298.4 0.0 reduce-scatter.5.cloned.1.call-update
  298.4 0.0 reduce-scatter.3.cloned.1.call-start
  298.4 0.7 reduce-scatter.3.cloned.1.call-update
  299.1 0.0 all-reduce.2.cloned.1.call-start
  299.2 127.3 %back.1 = (bf16[1024,1024]{1,0:T(8,128)(2,1)}, f32[1024,1024]{1,0:T(8,128)}, bf16[4,1024,1024]{2,1,0:T(8,128)(2,1)}, f32[8,1024]{1,0:T(8,128)}, bf16[8,256,1024]{2,1,0:T(8,128)(2,1)}) custom-call(bf16[8,256,1024]{2,1,0:T(8,128)(2,1)} %get-tuple-element.30.gback, bf16[8,256,1024]{2,1,0:T(8,128)(2,1)} %get-tuple-element.31.ret, ...), custom_call_target="tpu_custom_call" | custom-call | tf_op jit(solution)/shard_map/back/pallas_call | solution.py:410
  426.5 0.8 convert_element_type.12
  427.3 7.8 %pad_maximum_fusion = bf16[4104,1024]{1,0:T(8,128)(2,1)} fusion(bf16[8,1024]{1,0:T(8,128)(2,1)S(1)} %convert_element_type.12, bf16[4096,1024]{1,0:T(8,128)(2,1)} %bitcast.14), kind=kLoop, calls=%fused_computation | loop fusion | flops 16809984 | bytes 16809984 | tf_op jit(solution)/shard_map/concatenate | solution.py:432
  435.0 0.0 all-reduce.2.cloned.1.call-update
  435.1 0.0 all-gather.5.cloned.1.call-start
  435.1 0.0 reduce-scatter.5.cloned.1.call-done
  435.1 0.7 all-gather.5.cloned.1.call-update
  435.8 0.3 all-gather.3.cloned.1.call-start
  436.1 43.7 %reduce-scatter.3.cloned.1.call-done = bf16[1,1024,1024]{2,1,0:T(8,128)(2,1)} async-done(((bf16[1,1024,4096]{2,1,0:T(8,128)(2,1)}), bf16[1,1024,1024]{2,1,0:T(8,128)(2,1)}) %reduce-scatter.3.cloned.1.call-update) | async-done | bytes 2097168 | tf_op jit(solution)/shard_map/reduce_scatter | solution.py:429
  479.8 219.8 %all-reduce.2.cloned.1.call-done = bf16[4104,1024]{1,0:T(8,128)(2,1)} async-done(((bf16[4104,1024]{1,0:T(8,128)(2,1)}), bf16[4104,1024]{1,0:T(8,128)(2,1)}) %all-reduce.2.cloned.1.call-update) | async-done | bytes 8405008 | tf_op jit(solution)/shard_map/psum | solution.py:433
  699.6 1.4 fusion
  701.0 10.2 %fusion.1 = (f32[1024,1024]{1,0:T(8,128)}, f32[1024,1024]{1,0:T(8,128)}, f32[1024,1024]{1,0:T(8,128)}, f32[1024,1024]{1,0:T(8,128)}) fusion(bf16[4104,1024]{1,0:T(8,128)(2,1)} %all-reduce.2.cloned.1.call-done), kind=kLoop, calls=%fused_computation.2 | loop fusion | bytes 33554432 | tf_op jit(solution)/shard_map/slice | solution.py:434
  711.2 11.7 %convert_element_type.15 = f32[1,4096,1024]{2,1,0:T(8,128)} convert(bf16[1,4096,1024]{2,1,0:T(8,128)(2,1)} %all-gather.5.cloned.1.call-done) | non-fusion elementwise | flops 4194304 | bytes 25165824 | tf_op jit(solution)/shard_map/convert_element_type | solution.py:430
  722.9 12.0 %convert_element_type.14 = f32[1,1024,4096]{2,1,0:T(8,128)} convert(bf16[1,1024,4096]{2,1,0:T(8,128)(2,1)} %all-gather.3.cloned.1.call-done) | non-fusion elementwise | flops 4194304 | bytes 25165824 | tf_op jit(solution)/shard_map/convert_element_type | solution.py:431
  734.8 1.3 copy.24
  736.2 1.6 copy-done
  737.8 2.0 copy.25
  (6 shorter events, 0.0 us)
Async XLA Ops:
  8.0 427.1 %reduce-scatter.5.cloned.1.call-start = ((), (), s32[]{:S(2)}) async-start(), calls=%async_computation.5 | async-start | bytes 10485760 | tf_op jit(solution)/shard_map/reduce_scatter | solution.py:428
  298.4 181.4 %reduce-scatter.3.cloned.1.call-start = ((), (), s32[]{:S(2)}) async-start(), calls=%async_computation.3 | async-start | bytes 10485760 | tf_op jit(solution)/shard_map/reduce_scatter | solution.py:429
  299.1 400.5 %all-reduce.2.cloned.1.call-start = ((), (), s32[]{:S(2)}) async-start(), calls=%async_computation.2 | async-start | bytes 16809984 | tf_op jit(solution)/shard_map/psum | solution.py:433
  435.1 276.1 %all-gather.5.cloned.1.call-start = ((), (), s32[]{:S(2)}) async-start(), calls=%async_computation.6 | async-start | bytes 10485760 | tf_op jit(solution)/shard_map/all_gather | solution.py:430
  435.8 287.1 %all-gather.3.cloned.1.call-start = ((), (), s32[]{:S(2)}) async-start(), calls=%async_computation.4 | async-start | bytes 10485760 | tf_op jit(solution)/shard_map/all_gather | solution.py:431
  722.9 12.0 %copy-start.1 = (bf16[1024,1024]{1,0:T(8,128)(2,1)S(1)}, bf16[1024,1024]{1,0:T(8,128)(2,1)}, u32[]{:S(2)}) copy-start(bf16[1024,1024]{1,0:T(8,128)(2,1)} %get-tuple-element.62) | copy-start | bytes 6291460
  734.8 2.9 copy-start
Sparse Core Ops, SparseCore 0:
  298.5 100.9 reduce-scatter.4
  402.1 77.6 reduce-scatter.2
  481.4 58.5 all-gather.4
  541.5 58.4 all-gather.2
Sparse Core Ops, SparseCore 1:
  435.2 264.4 all-reduce.1

commit v2 on v1

--- a/solution.py
+++ b/solution.py
@@ -157,9 +157,9 @@
     slope=half+act*((1.0-th)*(SQ+3*SQ*0.044715*h2))
     return act,slope
 
-def expert_kernel(groups,cap,pack,cotarr,up,down,gback,ret,dup,ddown,act,
-                  arr,upv,downv,cotv,gpre,actb,gst,retb,stage,
-                  psend,precv,gsend,grecv,wsem,retsem,actsem,stsem,tsem):
+def expert_kernel(groups,cap,early,pack,cotarr,up,down,gback,ret,chipu,chipd,xgot,act,
+                  arr,upv,downv,cotv,gpre,actb,gst,retb,landu,landd,
+                  psend,precv,gsend,grecv,wsem,retsem,actsem,tsem,ssend,srecv,xsend,xrecv,csem):
     rows=groups*cap
     D,F=upv.shape
     FT=1024
@@ -169,7 +169,12 @@
         pl.semaphore_signal(barrier,inc=1,device_id={"expert":xor(me,i,groups)},device_id_type=MESH)
         return c
     lax.fori_loop(1,groups,greet,0)
-    pl.semaphore_wait(barrier,groups-1)
+    mine=lax.axis_index("replica")
+    core=mine%2
+    sibling=xor(mine,1,4); across=xor(mine,2,4)
+    for peer in (sibling,across):
+        pl.semaphore_signal(barrier,inc=1,device_id={"replica":peer},device_id_type=MESH)
+    pl.semaphore_wait(barrier,groups+1)
     def at(j): return pl.ds(pl.multiple_of(j*cap,cap),cap)
     def dispatch(j,i):
         return pltpu.make_async_remote_copy(src_ref=pack.at[j],dst_ref=arr.at[at(me)],send_sem=psend.at[i],recv_sem=precv.at[i],
@@ -189,76 +194,107 @@
     ccot=pltpu.make_async_copy(cotarr,cotv,wsem.at[1]); ccot.start()
     cdown=pltpu.make_async_copy(down,downv,wsem.at[2]); cdown.start()
     cup.wait(); ccot.wait(); cdown.wait()
-    def retcopy(j,b): return pltpu.make_async_copy(retb.at[b],ret.at[j],retsem.at[b])
-    def actcopy(j,b): return pltpu.make_async_copy(actb.at[b],act.at[at(j)],actsem.at[b])
+    def retcopy(j): return pltpu.make_async_copy(retb,ret.at[j],retsem)
+    def actcopy(j): return pltpu.make_async_copy(actb,act.at[at(j)],actsem)
+    def answer(i,c):
+        giveback(xor(me,i,groups),i).start()
+        return c
     def chunk(i,c):
         j=xor(me,i,groups)
-        b=i%2
         @pl.when(i==0)
         def _(): own.wait()
         @pl.when(i>0)
         def _(): dispatch(j,i).wait_recv()
-        @pl.when(i==half-1)
+        @pl.when(i==half-2)
         def _(): lax.fori_loop(half+half//2,groups,push,0)
-        @pl.when(i>=2)
+        @pl.when(i==groups-1)
         def _():
-            retcopy(j,b).wait(); actcopy(j,b).wait()
+            lax.fori_loop(half,groups-1,answer,0)
+            lax.fori_loop(1,half,answer,0)
+        @pl.when(i>=1)
+        def _(): actcopy(j).wait()
         def tile(t,c):
             s=pl.ds(pl.multiple_of(t*FT,FT),FT)
             h=dot(arr[at(j),:],upv[:,s])
             g=dg(cotv[j],downv[s,:],1,1)
             a,slope=gelu_pair(h)
-            actb[b,:,s]=a.astype(BF)
+            actb[:,s]=a.astype(BF)
             gpre[at(j),s]=(g*slope).astype(BF)
             return c
         lax.fori_loop(0,F//FT,tile,0)
         gst[at(j),:]=dg(gpre[at(j),:],upv[...],1,1).astype(BF)
-        @pl.when(i>0)
+        @pl.when(i==groups-1)
         def _(): giveback(j,i).start()
         @pl.when(i==0)
         def _(): pltpu.make_async_copy(gst.at[at(j)],gback.at[me],grecv.at[0]).start()
-        actcopy(j,b).start()
-        retb[b]=dot(actb[b],downv[...]).astype(BF)
-        retcopy(j,b).start()
+        actcopy(j).start()
+        @pl.when(i>=1)
+        def _(): retcopy(j).wait()
+        retb[...]=dot(actb[...],downv[...]).astype(BF)
+        retcopy(j).start()
         return c
     lax.fori_loop(0,groups,chunk,0)
-    for b in range(2):
-        retcopy(0,b).wait(); actcopy(0,b).wait()
+    retcopy(0).wait()
+    actcopy(0).wait()
     def atile(t,b): return pltpu.make_async_copy(act.at[:,pl.ds(pl.multiple_of(t*D,D),D)],downv.at[pl.ds(b*rows,rows)],tsem.at[b])
     atile(0,0).start(); atile(1,1).start()
     S=512
-    def upout(t,b): return pltpu.make_async_copy(stage.at[b],dup.at[:,pl.ds(pl.multiple_of(t*S,S),S)],stsem.at[b])
-    def dup_tile(t,c):
-        b=t%2
-        @pl.when(t>=2)
-        def _(): upout(t,b).wait()
-        def part(k,c):
-            r=pl.ds(pl.multiple_of(k*S,S),S)
-            stage[b,r,:]=dg(arr[:,r],gpre[:,pl.ds(pl.multiple_of(t*S,S),S)],0,0).astype(BF)
-            return c
-        lax.fori_loop(0,D//S,part,0)
-        upout(t,b).start()
-        return c
-    lax.fori_loop(0,F//S,dup_tile,0)
-    for b in range(2): upout(b,b).wait()
-    def downout(f,b): return pltpu.make_async_copy(upv.at[pl.ds(b*S,S),pl.ds(0,D)],ddown.at[pl.ds(pl.multiple_of(f*S,S),S)],stsem.at[b])
-    def ddown_tile(t,c):
-        tb=t%2
-        atile(t,tb).wait()
-        def part(p,c):
-            b=p%2
-            @pl.when(t*(D//S)+p>=2)
-            def _(): downout(0,b).wait()
-            a=downv[pl.ds(pl.multiple_of(tb*rows,rows),rows),pl.ds(pl.multiple_of(p*S,S),S)]
-            upv[pl.ds(pl.multiple_of(b*S,S),S),pl.ds(0,D)]=dg(a,cotv[...].reshape(rows,D),0,0).astype(BF)
-            downout(t*(D//S)+p,b).start()
-            return c
-        lax.fori_loop(0,D//S,part,0)
-        @pl.when(t+2<F//D)
-        def _(): atile(t+2,tb).start()
-        return c
-    lax.fori_loop(0,F//D,ddown_tile,0)
-    for b in range(2): downout(b,b).wait()
+    steps=F//(2*S)
+    def shared(n):
+        first=n*steps
+        chip,land=(chipu,landu) if n==0 else (chipd,landd)
+        def place(kind,b):
+            if n==0:
+                return upv.at[:,pl.ds((2*kind+b)*S,S)]
+            return upv.at[pl.ds(b*S,S),pl.ds(kind*D,D)]
+        def product(t,ref):
+            if n==0:
+                def part(k,c):
+                    r=pl.ds(pl.multiple_of(k*S,S),S)
+                    ref[r,:]=dg(arr[:,r],gpre[:,pl.ds(pl.multiple_of(t*S,S),S)],0,0).astype(BF)
+                    return c
+                lax.fori_loop(0,D//S,part,0)
+            else:
+                tb=(t//2)%2; Q=S//2
+                def part(k,c):
+                    a=downv[pl.ds(pl.multiple_of(tb*rows,rows),rows),pl.ds(pl.multiple_of((t%2)*S+k*Q,Q),Q)]
+                    ref[pl.ds(pl.multiple_of(k*Q,Q),Q),:]=dg(a,cotv[...].reshape(rows,D),0,0).astype(BF)
+                    return c
+                lax.fori_loop(0,2,part,0)
+        def tosib(s,b):
+            return pltpu.make_async_remote_copy(src_ref=place(0,b),dst_ref=land.at[s],send_sem=ssend.at[first+s],recv_sem=srecv.at[first+s],
+                device_id={"replica":sibling},device_id_type=MESH)
+        def tochip(s,b): return pltpu.make_async_copy(place(1,b),chip.at[s],csem.at[first+s])
+        def finish(s):
+            tosib(s,s%2).wait_recv()
+            ref=place(1,s%2)
+            def add(k,c):
+                r=pl.ds(pl.multiple_of(k*128,128),128)
+                ref[r,:]=(ref[r,:].astype(F32)+land[s,r,:].astype(F32)).astype(BF)
+                return c
+            lax.fori_loop(0,ref.shape[0]//128,add,0)
+            tochip(s,s%2).start()
+        def leave(s):
+            tochip(s,s%2).wait()
+            if first+s<early: toacross(s).start()
+        for s in range(steps):
+            b=s%2
+            if n==1: atile(s,b).wait()
+            if s>=2: tosib(s-2,b).wait_send()
+            product(2*s+1-core,place(0,b))
+            tosib(s,b).start()
+            if s>=1: finish(s-1)
+            product(2*s+core,place(1,b))
+            if n==1 and s+2<steps: atile(s+2,b).start()
+            if s>=1: leave(s-1)
+        finish(steps-1)
+        for s in range(max(0,steps-2),steps): tosib(s,s%2).wait_send()
+        leave(steps-1)
+    def toacross(s):
+        return pltpu.make_async_remote_copy(src_ref=chipu.at[s],dst_ref=xgot.at[s],send_sem=xsend.at[s],recv_sem=xrecv.at[s],
+            device_id={"replica":across},device_id_type=MESH)
+    shared(0)
+    shared(1)
     pltpu.make_async_copy(gst.at[at(me)],gback.at[me],grecv.at[0]).wait()
     def finish(i,c):
         j=xor(me,i,groups)
@@ -266,20 +302,24 @@
         giveback(j,i).wait()
         return c
     lax.fori_loop(1,groups,finish,0)
-
-def expert(pack,cotarr,up,down):
+    for s in range(early): toacross(s).wait()
+
+def expert(pack,cotarr,up,down,early):
     groups,cap,D=pack.shape
     F=up.shape[1]; rows=groups*cap
+    S=512; steps=F//(2*S)
     A=pl.BlockSpec(memory_space=pl.ANY)
     sd=jax.ShapeDtypeStruct
     DMA=pltpu.SemaphoreType.DMA
-    return pl.pallas_call(functools.partial(expert_kernel,groups,cap),
-      in_specs=[A]*4,out_specs=[A]*5,
-      out_shape=[sd((groups,cap,D),BF)]*2+[sd((D,F),BF),sd((F,D),BF),sd((rows,F),BF)],
+    su=sd((steps,D,S),BF); sdn=sd((steps,S,D),BF)
+    return pl.pallas_call(functools.partial(expert_kernel,groups,cap,early),
+      in_specs=[A]*4,out_specs=[A]*6,
+      out_shape=[sd((groups,cap,D),BF)]*2+[su,sdn,sd((early,D,S),BF),sd((rows,F),BF)],
       scratch_shapes=[pltpu.VMEM((rows,D),BF),pltpu.VMEM((D,F),BF),pltpu.VMEM((F,D),BF),pltpu.VMEM((groups,cap,D),BF),pltpu.VMEM((rows,F),BF),
-         pltpu.VMEM((2,cap,F),BF),pltpu.VMEM((rows,D),BF),pltpu.VMEM((2,cap,D),BF),pltpu.VMEM((2,D,512),BF),
-         DMA((groups,)),DMA((groups,)),DMA((groups,)),DMA((groups,)),DMA((3,)),DMA((2,)),DMA((2,)),DMA((2,)),DMA((2,))],
-      compiler_params=pltpu.CompilerParams(vmem_limit_bytes=63*2**20,collective_id=1,has_side_effects=True),
+         pltpu.VMEM((cap,F),BF),pltpu.VMEM((rows,D),BF),pltpu.VMEM((cap,D),BF),pltpu.VMEM((steps,D,S),BF),pltpu.VMEM((steps,S,D),BF),
+         DMA((groups,)),DMA((groups,)),DMA((groups,)),DMA((groups,)),DMA((3,)),DMA,DMA,DMA((2,)),
+         DMA((2*steps,)),DMA((2*steps,)),DMA((early,)),DMA((early,)),DMA((2*steps,))],
+      compiler_params=pltpu.CompilerParams(vmem_limit_bytes=63*2**20+2**19,collective_id=1,has_side_effects=True),
       name="experts")(pack,cotarr,up,down)
 
 
@@ -308,24 +348,33 @@
             dqs[i]=part if dqs[i] is None else dqs[i]+part
     return [(x*scale).astype(BF).T for x in dqs],[x.astype(BF) for x in dks],[x.astype(BF) for x in dvs]
 
-def back_kernel(groups,cap,block,
-        gback,ret,slot,hid,cot,tok,normed,q,k,v,att,lse,g1,g2,wq,wk,wv,wo,
-        output,gtok,dw,dgain,rarr,
-        vslots,vhid,vcot,vtok,vnormed,vq,vk,vv,vatt,vwq,vwk,vwv,vwo,ghl,datt,dq,dk,dv,
-        isem,ssem,rsem,lsem):
-    T,D=vtok.shape
+def back_kernel(groups,cap,block,early,
+        gback,ret,slot,hid,cot,tok,normed,q,k,v,att,lse,g1,g2,wq,wk,wv,wo,chipu,chipd,xgot,
+        output,gtok,dw,dgain,dup,ddown,rarr,xu,xd,
+        vslots,vhid,vcot,vnormed,vq,vk,vv,vatt,vwo,ghl,datt,dq,dk,dv,vgt,dwv,rbuf,gbuf,
+        isem,ssem,rsem,lsem,dsend,drecv,osem,xsend,xrecv,fsem,fout,fsend,frecv,gsend,grecv,credit):
+    T,D=vnormed.shape
     R=256
+    S=chipu.shape[2]
+    steps=chipu.shape[0]
+    parts=4
+    W=D//parts
     rows=groups*cap
     me=lax.axis_index("expert")
+    mine=lax.axis_index("replica")
+    core=mine%2
+    sibling=xor(mine,1,4); across=xor(mine,2,4)
     barrier=pltpu.get_barrier_semaphore()
     def greet(i,c):
         pl.semaphore_signal(barrier,inc=1,device_id={"expert":xor(me,i,groups)},device_id_type=MESH)
         return c
     lax.fori_loop(1,groups,greet,0)
+    for peer in (sibling,across):
+        pl.semaphore_signal(barrier,inc=1,device_id={"replica":peer},device_id_type=MESH)
     copies=[pltpu.make_async_copy(a,b,isem.at[i]) for i,(a,b) in enumerate(
-        ((gback,vslots),(hid,vhid),(cot,vcot),(wo,vwo),(att,vatt),(q,vq),(k,vk),(v,vv),(normed,vnormed),(wq,vwq),(wk,vwk),(wv,vwv),(tok,vtok)))]
+        ((gback,vslots),(hid,vhid),(cot,vcot),(wo,vwo),(att,vatt),(q,vq),(k,vk),(v,vv),(normed,vnormed)))]
     for c in copies: c.start()
-    pl.semaphore_wait(barrier,groups-1)
+    pl.semaphore_wait(barrier,groups+1)
     def send(i):
         j=xor(me,i,groups)
         return pltpu.make_async_remote_copy(src_ref=ret.at[j],dst_ref=rarr.at[me],send_sem=ssem.at[i],recv_sem=rsem.at[i],
@@ -335,6 +384,93 @@
         return c
     lax.fori_loop(1,groups,push,0)
     own=pltpu.make_async_copy(ret.at[me],rarr.at[me],lsem); own.start()
+    def toacross(n,s):
+        src,dst=(chipu.at[s],xu.at[s-early]) if n==0 else (chipd.at[s],xd.at[s])
+        return pltpu.make_async_remote_copy(src_ref=src,dst_ref=dst,send_sem=xsend.at[n,s],recv_sem=xrecv.at[n,s],
+            device_id={"replica":across},device_id_type=MESH)
+    late=[(0,s) for s in range(early,steps)]+[(1,s) for s in range(steps)]
+    def spare(n,i):
+        return vatt.at[:,pl.ds(i*S,S)] if n==0 else vnormed.at[pl.ds(i*S,S)]
+    def finalize(n,s,got):
+        a,b=spare(n,0),spare(n,1)
+        l1=pltpu.make_async_copy((chipu if n==0 else chipd).at[s],a,fsem.at[0]); l1.start()
+        l2=pltpu.make_async_copy(got,b,fsem.at[1]); l2.start()
+        l1.wait(); l2.wait()
+        def add(i,c):
+            r=pl.ds(pl.multiple_of(i*128,128),128)
+            a[r,:]=(a[r,:].astype(F32)+b[r,:].astype(F32)).astype(BF)
+            return c
+        lax.fori_loop(0,a.shape[0]//128,add,0)
+        keep,share=leaving(n,s)
+        keep.start(); share.start()
+    def leaving(n,s):
+        a=spare(n,0)
+        d=pl.ds(pl.multiple_of((2*s+core)*S,S),S)
+        there=dup.at[:,d] if n==0 else ddown.at[d]
+        return (pltpu.make_async_copy(a,there,fout.at[n]),
+            pltpu.make_async_remote_copy(src_ref=a,dst_ref=there,send_sem=fsend.at[n,s],recv_sem=frecv.at[n,s],
+                device_id={"replica":sibling},device_id_type=MESH))
+    def left(n,s):
+        keep,share=leaving(n,s)
+        keep.wait(); share.wait_send()
+    for n,s in late[:2]: toacross(n,s).start()
+    bits=[("replica",mine,1)]+[("expert",me,1<<b) for b in range(groups.bit_length()-1)]
+    H=len(bits)
+    base=[0]; other=[]; peers=[]
+    for i,(axis,index,step) in enumerate(bits):
+        n=D>>(i+1)
+        bit=(index//step)%2
+        other.append(base[-1]+(1-bit)*n)
+        base.append(base[-1]+bit*n)
+        peers.append({axis:index+step-2*step*bit})
+    size=[D>>(i+1) for i in range(H)]+[D>>H]
+    offset=[D-(D>>i) for i in range(H+1)]
+    def piece(ref,c,first,n):
+        return ref.at[:,pl.ds(pl.multiple_of(first,n),n),pl.ds(pl.multiple_of(c*W,W),W)]
+    def move(c,k):
+        if k<H:
+            src=piece(dwv,c,other[k],size[k]); dst=piece(rbuf,c,offset[k],size[k]); peer=peers[k]
+        elif k==H:
+            src=piece(dwv,c,base[H],size[H]); dst=piece(rbuf,c,offset[H],size[H]); peer={"replica":across}
+        else:
+            i=2*H-k
+            src=dst=piece(dwv,c,base[i+1],size[i]); peer=peers[i]
+        return pltpu.make_async_remote_copy(src_ref=src,dst_ref=dst,send_sem=dsend.at[c,k],recv_sem=drecv.at[c,k],device_id=peer,device_id_type=MESH)
+    def gather_in(c,k):
+        first=base[min(k+1,H)]; n=size[k]
+        m=min(n,64)
+        cols=pl.ds(pl.multiple_of(c*W,W),W)
+        def add(i,z):
+            r=pl.ds(pl.multiple_of(first+i*m,m),m)
+            o=pl.ds(pl.multiple_of(offset[k]+i*m,m),m)
+            for x in range(4):
+                dwv[x,r,cols]=(dwv[x,r,cols].astype(F32)+rbuf[x,o,cols].astype(F32)).astype(BF)
+            return z
+        lax.fori_loop(0,n//m,add,0)
+    def out_dense(c):
+        cols=pl.ds(pl.multiple_of(c*W,W),W)
+        return pltpu.make_async_copy(dwv.at[:,:,cols],dw.at[:,:,cols],osem.at[c])
+    K=2*H+2
+    def progress(t):
+        for k in range(K-1,-1,-1):
+            c=t-k
+            @pl.when((c>=0)&(c<parts))
+            def _():
+                if k>0:
+                    move(c,k-1).wait()
+                    if k<=H: pl.semaphore_signal(credit.at[c,k-1],inc=1,device_id=peers[k-1],device_id_type=MESH)
+                if 0<k<=H+1: gather_in(c,k-1)
+                if H<k<K-1: pl.semaphore_wait(credit.at[c,2*H-k],1)
+                if k<K-1: move(c,k).start()
+                else: out_dense(c).start()
+    gbits=peers+[{"replica":across}]
+    def gain_move(j):
+        return pltpu.make_async_remote_copy(src_ref=dgain,dst_ref=gbuf.at[j],send_sem=gsend.at[j],recv_sem=grecv.at[j],device_id=gbits[j],device_id_type=MESH)
+    def gain_step(j):
+        if j>0:
+            gain_move(j-1).wait()
+            dgain[...]=dgain[...]+gbuf[j-1]
+        if j<len(gbits): gain_move(j).start()
     def gathered(r):
         col=jnp.broadcast_to(slot[:,r],(128,R)).T[:,:1]
         ids=lax.broadcasted_iota(jnp.int32,(R,rows),1).astype(F32)
@@ -348,20 +484,21 @@
         m=gs*g2[...]
         dgain[1:2,:]+=jnp.sum(gs*u,axis=0,keepdims=True)
         gh=vcot[r,:].astype(F32)+inv*(m-jnp.mean(m,axis=-1,keepdims=True)-u*jnp.mean(m*u,axis=-1,keepdims=True))
-        gtok[r,:]=gh
+        vgt[r,:]=gh
         ghl[r,:]=gh.astype(BF)
         return c
     lax.fori_loop(0,T//R,norm_two,0)
+    again=pltpu.make_async_copy(tok,vcot,isem.at[2]); again.start()
     for c in copies[3:5]: c.wait()
     def outproj(i,c):
         s=pl.ds(pl.multiple_of(i*R,R),R)
         datt[s,:]=dg(vwo[s,:],ghl[...],1,1).astype(BF)
-        dw[3,s,:]=dot(vatt[s,:],ghl[...]).astype(BF)
+        dwv[3,s,:]=dot(vatt[s,:],ghl[...]).astype(BF)
         return c
     lax.fori_loop(0,D//R,outproj,0)
     for c in copies[5:]: c.wait()
-    def pair(h,c):
-        w=2*HEAD_DIM
+    w=2*HEAD_DIM
+    def pair(h):
         col=pl.ds(pl.multiple_of(h*w,w),w)
         res=[]
         for a in range(2):
@@ -370,50 +507,110 @@
         for ref,x,y in zip((dq,dk,dv),*res):
             for i in range(T//block):
                 ref[i*block:(i+1)*block,col]=jnp.concatenate([x[i],y[i]],axis=1)
-        return c
-    lax.fori_loop(0,D//(2*HEAD_DIM),pair,0)
-    def wgrad(i,c):
-        s=pl.ds(pl.multiple_of(i*R,R),R)
-        for n,x in enumerate((dq,dk,dv)):
-            dw[n,s,:]=dg(vnormed[:,s],x[...],0,0).astype(BF)
-        return c
-    lax.fori_loop(0,D//R,wgrad,0)
-    def norm_one(i,c):
-        r=pl.ds(pl.multiple_of(i*R,R),R)
-        gn=dg(dq[r,:],vwq[...],1,1)+dg(dk[r,:],vwk[...],1,1)+dg(dv[r,:],vwv[...],1,1)
-        u,inv=norm_stats(vtok[r,:].astype(F32))
-        m=gn*g1[...]
-        dgain[0:1,:]+=jnp.sum(gn*u,axis=0,keepdims=True)
-        gtok[r,:]+=inv*(m-jnp.mean(m,axis=-1,keepdims=True)-u*jnp.mean(m*u,axis=-1,keepdims=True))
-        return c
-    lax.fori_loop(0,T//R,norm_one,0)
+    loads=[pltpu.make_async_copy(a,b,isem.at[5+i]) for i,(a,b) in enumerate(((wq,vq),(wk,vk),(wv,vv)))]
+    def time(t,c):
+        @pl.when(t<parts)
+        def _():
+            per=D//w//parts
+            def one(i,c):
+                pair(t*per+i)
+                return c
+            lax.fori_loop(0,per,one,0)
+            cols=pl.ds(pl.multiple_of(t*W,W),W)
+            for n,x in enumerate((dq,dk,dv)):
+                def rowpart(i,c):
+                    s=pl.ds(pl.multiple_of(i*R,R),R)
+                    dwv[n,s,cols]=dg(vnormed[:,s],x[:,cols],0,0).astype(BF)
+                    return c
+                lax.fori_loop(0,D//R,rowpart,0)
+        @pl.when(t==parts-1)
+        def _():
+            for x in loads: x.start()
+        @pl.when(t==parts)
+        def _():
+            again.wait()
+            for x in loads: x.wait()
+        @pl.when((t>=parts)&(t<2*parts))
+        def _():
+            n=T//parts
+            r=pl.ds(pl.multiple_of((t-parts)*n,n),n)
+            gn=dg(dq[r,:],vq[...],1,1)+dg(dk[r,:],vk[...],1,1)+dg(dv[r,:],vv[...],1,1)
+            u,inv=norm_stats(vcot[r,:].astype(F32))
+            m=gn*g1[...]
+            dgain[0:1,:]+=jnp.sum(gn*u,axis=0,keepdims=True)
+            vgt[r,:]+=inv*(m-jnp.mean(m,axis=-1,keepdims=True)-u*jnp.mean(m*u,axis=-1,keepdims=True))
+        progress(t)
+        for i,at in ((2,1),(4,4)):
+            @pl.when(t==at)
+            def _():
+                for n,s in late[i:i+2]: toacross(n,s).start()
+        @pl.when(t==2*parts)
+        def _(): pltpu.make_async_copy(vgt,gtok,isem.at[0]).start()
+        for j in range(ingain):
+            @pl.when(t==2*parts+j)
+            def _(): gain_step(j)
+        for p,(n,s) in enumerate(order[:inloop]):
+            @pl.when(t==parts+1+p)
+            def _(): settle(p)
+        return c
+    order=[(0,s) for s in range(steps)]+[(1,s) for s in range(steps)]
+    def settle(p):
+        n,s=order[p]
+        if p>0 and order[p-1][0]==n: left(n,s-1)
+        if n==0 and s<early:
+            finalize(n,s,xgot.at[s])
+        else:
+            toacross(n,s).wait()
+            finalize(n,s,xu.at[s-early] if n==0 else xd.at[s])
+        if p>0 and order[p-1][0]!=n: left(*order[p-1])
+    last=parts+K-1
+    inloop=steps+steps//2
+    ingain=min(len(gbits)+1,last-2*parts)
+    for n,s in late[6:]: toacross(n,s).start()
+    lax.fori_loop(0,last,time,0)
+    for j in range(ingain,len(gbits)+1): gain_step(j)
     own.wait()
     def finish(i,c):
         send(i).wait()
         return c
     lax.fori_loop(1,groups,finish,0)
-    load=pltpu.make_async_copy(rarr,vslots,lsem); load.start(); load.wait()
+    load=pltpu.make_async_copy(rarr,vslots,lsem); load.start()
+    for p in range(inloop,len(order)): settle(p)
+    load.wait()
     def final(i,c):
         r=pl.ds(pl.multiple_of(i*R,R),R)
-        output[r,:]=(vhid[r,:]+gathered(r)).astype(BF)
+        ghl[r,:]=(vhid[r,:]+gathered(r)).astype(BF)
         return c
     lax.fori_loop(0,T//R,final,0)
-
-def back(gback,ret,slot,hid,cot,tok,normed,q,k,v,att,lse,g1,g2,wq,wk,wv,wo,block=256):
+    last_out=pltpu.make_async_copy(ghl,output,isem.at[1]); last_out.start()
+    left(*order[-1])
+    for n,s in order: leaving(n,s)[1].wait_recv()
+    for c in range(parts): out_dense(c).wait()
+    pltpu.make_async_copy(vgt,gtok,isem.at[0]).wait()
+    last_out.wait()
+
+def back(gback,ret,slot,hid,cot,tok,normed,q,k,v,att,lse,g1,g2,wq,wk,wv,wo,chipu,chipd,xgot,block=256):
     groups,cap,D=ret.shape
     T=tok.shape[0]
+    steps,_,S=chipu.shape
+    early=xgot.shape[0]
+    F=2*steps*S
+    H=groups.bit_length()
     V=pl.BlockSpec(memory_space=pltpu.VMEM)
     A=pl.BlockSpec(memory_space=pl.ANY)
     sd=jax.ShapeDtypeStruct
     DMA=pltpu.SemaphoreType.DMA
-    dn=(D,T)
-    return pl.pallas_call(functools.partial(back_kernel,groups,cap,block),
-      in_specs=[A,A,V]+[A]*8+[V]*3+[A]*4,out_specs=[V]*4+[A],
-      out_shape=[sd((T,D),BF),sd((T,D),F32),sd((4,D,D),BF),sd((8,D),F32),sd((groups,cap,D),BF)],
-      scratch_shapes=[pltpu.VMEM((groups,cap,D),BF),pltpu.VMEM((T,D),F32)]+[pltpu.VMEM((T,D),BF)]*3+[pltpu.VMEM((D,T),BF)]*4+[pltpu.VMEM((D,D),BF)]*4
-         +[pltpu.VMEM((T,D),BF),pltpu.VMEM((D,T),BF)]+[pltpu.VMEM((T,D),BF)]*3+[DMA((13,)),DMA((groups,)),DMA((groups,)),DMA],
-      compiler_params=pltpu.CompilerParams(vmem_limit_bytes=63*2**20,collective_id=2,has_side_effects=True),
-      name="back")(gback,ret,slot,hid,cot,tok,normed,q,k,v,att,lse,g1,g2,wq,wk,wv,wo)
+    M=lambda *s: pltpu.VMEM(s,BF)
+    return pl.pallas_call(functools.partial(back_kernel,groups,cap,block,early),
+      in_specs=[A,A,V]+[A]*8+[V]*3+[A]*7,out_specs=[A]*3+[V]+[A]*5,
+      out_shape=[sd((T,D),BF),sd((T,D),F32),sd((4,D,D),BF),sd((8,D),F32),sd((D,F),BF),sd((F,D),BF),sd((groups,cap,D),BF),
+         sd((steps-early,D,S),BF),sd((steps,S,D),BF)],
+      scratch_shapes=[M(groups,cap,D),pltpu.VMEM((T,D),F32),M(T,D),M(T,D),M(D,T),M(D,T),M(D,T),M(D,T),M(D,D),M(T,D),M(D,T),M(T,D),M(T,D),M(T,D),
+         pltpu.VMEM((T,D),F32),M(4,D,D),M(4,D,D),pltpu.VMEM((H+1,8,D),F32),
+         DMA((9,)),DMA((groups,)),DMA((groups,)),DMA,DMA((4,2*H+1)),DMA((4,2*H+1)),DMA((4,)),DMA((2,steps)),DMA((2,steps)),DMA((2,)),DMA((2,)),DMA((2,steps)),DMA((2,steps)),
+         DMA((H+1,)),DMA((H+1,)),pltpu.SemaphoreType.REGULAR((4,H))],
+      compiler_params=pltpu.CompilerParams(vmem_limit_bytes=63*2**20+2**19,collective_id=2,has_side_effects=True),
+      name="back")(gback,ret,slot,hid,cot,tok,normed,q,k,v,att,lse,g1,g2,wq,wk,wv,wo,chipu,chipd,xgot)
 
 
 def per_device(tokens,routes,gain_one,query_weight,key_weight,value_weight,out_weight,gain_two,up_weight,down_weight,cotangent):
@@ -423,18 +620,10 @@
     g1=gain_one.reshape(1,D); g2=gain_two.reshape(1,D)
     weights=(query_weight,key_weight,value_weight,out_weight)
     normed,q,k,v,att,lse,hid,pack,slot,cotarr=front(tokens,routes.reshape(1,T),cotangent,g1,g2,*weights,groups,cap)
-    gback,ret,dup,ddown,_=expert(pack,cotarr,up_weight[0],down_weight[0])
-    output,gtok,dw,dgain,_=back(gback,ret,slot,hid,cotangent,tokens,normed,q,k,v,att,lse,g1,g2,*weights)
-    sdown=lax.psum_scatter(ddown[None],"replica",scatter_dimension=1,tiled=True)
-    sup=lax.psum_scatter(dup[None],"replica",scatter_dimension=2,tiled=True)
-    gdown=lax.all_gather(sdown,"replica",axis=1,tiled=True).astype(F32)
-    gup=lax.all_gather(sup,"replica",axis=2,tiled=True).astype(F32)
-    packed=jnp.concatenate([dw.reshape(4*D,D),dgain.astype(BF)],axis=0)
-    total=lax.psum(packed,("expert","replica")).astype(F32)
-    ws=[total[i*D:(i+1)*D] for i in range(4)]
-    return (output,gtok,total[4*D],*ws,total[4*D+1],gup,gdown)
-
-
+    gback,ret,chipu,chipd,xgot,_=expert(pack,cotarr,up_weight[0],down_weight[0],2)
+    output,gtok,dw,dgain,dup,ddown,_,_,_=back(gback,ret,slot,hid,cotangent,tokens,normed,q,k,v,att,lse,g1,g2,*weights,chipu,chipd,xgot)
+    ws=[dw[i].astype(F32) for i in range(4)]
+    return (output,gtok,dgain[0],*ws,dgain[1],dup.astype(F32)[None],ddown.astype(F32)[None])
 def solution(mesh):
     rows=P(("expert","replica"),None)
     each=P("expert",None,None)

time: 747 us -> 605 us (0.81); the launches traced: 747 us -> 597 us
  waiting for transfers between devices: 265 us -> 0 us
  Pallas kernels: 418 us -> 555 us
  between operations: 15.3 us -> 1.11 us
  local copies, waits for them, and re-layouts: 16.5 us -> 6.4 us
    psum x1 -> x0, waiting for transfers between devices: 220 us -> none  [per_device(): total = lax.psum(packed, ('expert', 'replica')).astype(F32)]
    pallas_call x2, Pallas kernels: 300 us -> 438 us  [the longest x1 252 us: back(): pl.pallas_call(functools.partial(back_kernel, groups, cap, block, early),...]
    reduce_scatter x2 -> x0, waiting for transfers between devices: 43.7 us -> none  [the longest x1 43.7 us: per_device(): lax.psum_scatter(dup[None], 'replica', scatter_dimension=2, tiled=True)]
    broadcast_in_dim x0 -> x2, other arithmetic: none -> 23.5 us  [the longest x1 11.8 us: per_device(): dup.astype(F32)[None]]
    convert_element_type x3 -> x1, other arithmetic: 24.4 us -> 10.3 us  [per_device(): ws = [dw[i].astype(F32) for i in range(4)]]
    slice x2 -> x1, local copies, waits for them, and re-layouts: 11.6 us -> 1.44 us  [per_device(): dgain[1]]
    concatenate x1 -> x0, other arithmetic: 7.76 us -> none  [per_device(): packed = jnp.concatenate([dw.reshape(4 * D, D), dgain.astype(BF)], axis=0)]
  transfers between devices with their start and end apart: 5 -> 0, of which waited for: 2 -> 0; matrix products, arithmetic and copies ran while one was open for 4% -> 0% of each run, Pallas kernels for 17% -> 0%
where the time goes in v2:
time: 605 us; the launch traced here: 597 us
  Pallas kernels  555 us (92%)
  other arithmetic  33.8 us (6%)
  local copies, waits for them, and re-layouts  6.4 us (1%)
    pallas_call x1, Pallas kernels, back(): pl.pallas_call(functools.partial(back_kernel, groups, cap, block, early),...  252 us
    pallas_call x1, Pallas kernels, expert(): pl.pallas_call(functools.partial(expert_kernel, groups, cap, early), in_s...  186 us
    pallas_call x1, Pallas kernels, front(): pl.pallas_call(functools.partial(front_kernel, groups, cap, block), in_sp...  118 us

profile of v2, /device:TPU:0, one launch (start us, length us, event | category | flops | bytes accessed | tf_op | source)
XLA Modules:
  0.0 596.6 jit_solution(6907585611491957432)
XLA Ops:
  0.6 117.6 %front.1 = (bf16[1024,1024]{1,0:T(8,128)(2,1)}, bf16[1024,1024]{1,0:T(8,128)(2,1)}, bf16[1024,1024]{1,0:T(8,128)(2,1)}, bf16[1024,1024]{1,0:T(8,128)(2,1)}, bf16...) custom-call(bf16[1024,1024]{1,0:T(8,128)(2,1)} %tok.3, ...), custom_call_target="tpu_custom_call" | custom-call | tf_op jit(solution)/shard_map/front/pallas_call | solution.py:133
  118.2 185.7 %experts.1 = (bf16[8,256,1024]{2,1,0:T(8,128)(2,1)}, bf16[8,256,1024]{2,1,0:T(8,128)(2,1)}, bf16[4,1024,512]{2,1,0:T(8,128)(2,1)}, bf16[4,512,1024]{2,1,0:T(8,12...) custom-call(bf16[8,256,1024]{2,1,0:T(8,128)(2,1)} %get-tuple-element.31.pack, ...), custom_call_target="tpu_custom_call" | custom-call | tf_op jit(solution)/shard_map/experts/pallas_call | solution.py:315
  304.0 251.9 %back.1 = (bf16[1024,1024]{1,0:T(8,128)(2,1)}, f32[1024,1024]{1,0:T(8,128)}, bf16[4,1024,1024]{2,1,0:T(8,128)(2,1)}, f32[8,1024]{1,0:T(8,128)}, bf16[1024,4096]{...) custom-call(bf16[8,256,1024]{2,1,0:T(8,128)(2,1)} %get-tuple-element, ...), custom_call_target="tpu_custom_call" | custom-call | tf_op jit(solution)/shard_map/back/pallas_call | solution.py:604
  555.9 1.4 fusion
  557.4 11.8 %bitcast_convert_fusion.1 = f32[1,1024,4096]{2,1,0:T(8,128)} fusion(bf16[1024,4096]{1,0:T(8,128)(2,1)} %get-tuple-element.50), kind=kLoop, calls=%fused_computation.1 | loop fusion | flops 4194304 | bytes 25165824 | tf_op jit(solution)/shard_map/broadcast_in_dim | solution.py:626
  569.2 11.7 %bitcast_convert_fusion = f32[1,4096,1024]{2,1,0:T(8,128)} fusion(bf16[4096,1024]{1,0:T(8,128)(2,1)} %get-tuple-element.51), kind=kLoop, calls=%fused_computation | loop fusion | flops 4194304 | bytes 25165824 | tf_op jit(solution)/shard_map/broadcast_in_dim | solution.py:626
  580.9 0.0 copy-start.1
  580.9 10.3 %bitcast_convert_fusion.2 = (f32[1024,1024]{1,0:T(8,128)}, f32[1024,1024]{1,0:T(8,128)}, f32[1024,1024]{1,0:T(8,128)}, f32[1024,1024]{1,0:T(8,128)}) fusion(bf16[4,1024,1024]{2,1,0:T(8,128)(2,1)} %get-tuple-element.49), kind=kLoop, calls=%fused_computation.2 | loop fusion | flops 4194304 | bytes 25165824 | tf_op jit(solution)/shard_map/convert_element_type | solution.py:625
  591.2 0.0 copy-start
  591.2 0.0 copy-done.1
  591.2 1.3 copy.23
  592.5 1.6 copy-done
  594.1 2.0 copy.24
Async XLA Ops:
  580.9 10.3 %copy-start.1 = (bf16[1024,1024]{1,0:T(8,128)(2,1)S(1)}, bf16[1024,1024]{1,0:T(8,128)(2,1)}, u32[]{:S(2)}) copy-start(bf16[1024,1024]{1,0:T(8,128)(2,1)} %get-tuple-element.68) | copy-start | bytes 6291460
  591.2 2.9 copy-start

commit v3 on v2

--- a/solution.py
+++ b/solution.py
@@ -56,9 +56,12 @@
     ids=(lax.broadcasted_iota(jnp.int32,(count,slot.shape[1]),0)+first).astype(F32)
     return jnp.where(ids==slot,1.0,0.0).astype(BF)
 
-def front_kernel(groups,cap,block,tok,rt,cot,g1,g2,wq,wk,wv,wo,
-                 normed,q,k,v,att,lse,hid,pack,slot,cotarr,
-                 cpack,n2,ssem,rsem,lsem):
+def front_kernel(groups,cap,block,htok,rt,cot,g1,g2,hwq,hwk,hwv,hwo,
+                 hnormed,hq,hk,hv,hatt,lse,hhid,hpack,slot,cotarr,
+                 tok,wq,wk,wv,wo,normed,q,k,v,att,hid,pack,cpack,n2,ssem,rsem,lsem,isem,osem):
+    loads=[pltpu.make_async_copy(a,b,isem.at[i]) for i,(a,b) in enumerate(((htok,tok),(hwq,wq),(hwk,wk),(hwv,wv),(hwo,wo)))]
+    for c in loads: c.start()
+    stores=[pltpu.make_async_copy(a,b,osem.at[i]) for i,(a,b) in enumerate(((normed,hnormed),(q,hq),(k,hk),(v,hv),(att,hatt),(hid,hhid),(pack,hpack)))]
     T,D=tok.shape
     R=256
     me=lax.axis_index("expert")
@@ -85,18 +88,21 @@
     cpack[me]=dot(onehot_rows(slots,me*cap,cap),cot[...]).astype(BF)
     own=pltpu.make_async_copy(cpack.at[me],cotarr.at[me],lsem)
     own.start()
+    for c in loads: c.wait()
     def norm_one(i,c):
         r=pl.ds(pl.multiple_of(i*R,R),R)
         u,_=norm_stats(tok[r,:].astype(F32))
-        normed[r,:]=(u*g1[...]).astype(BF)
+        normed[:,r]=(u*g1[...]).astype(BF).T
         return c
     lax.fori_loop(0,T//R,norm_one,0)
+    stores[0].start()
     def proj(i,c):
         s=pl.ds(pl.multiple_of(i*R,R),R)
         for w,o in ((wq,q),(wk,k),(wv,v)):
-            o[s,:]=dg(w[:,s],normed[...],0,1).astype(BF)
+            o[s,:]=dg(w[:,s],normed[...],0,0).astype(BF)
         return c
     lax.fori_loop(0,D//R,proj,0)
+    for c in stores[1:4]: c.start()
     def head(h,c):
         s=pl.ds(pl.multiple_of(h*HEAD_DIM,HEAD_DIM),HEAD_DIM)
         outs,lses=fwd_head(q[s,:],k[s,:],v[s,:],block)
@@ -104,6 +110,7 @@
         lse[pl.ds(h,1),:]=jnp.concatenate(lses,axis=1)
         return c
     lax.fori_loop(0,D//HEAD_DIM,head,0)
+    stores[4].start()
     def out(i,c):
         r=pl.ds(pl.multiple_of(i*R,R),R)
         h=tok[r,:].astype(F32)+dg(att[:,r],wo[...],0,0)
@@ -112,11 +119,14 @@
         n2[r,:]=(u*g2[...]).astype(BF)
         return c
     lax.fori_loop(0,T//R,out,0)
+    stores[5].start()
     def packing(i,c):
         pack[i]=dot(onehot_rows(slots,i*cap,cap),n2[...]).astype(BF)
         return c
     lax.fori_loop(0,groups,packing,0)
+    stores[6].start()
     own.wait()
+    for c in stores: c.wait()
     def finish(i,c):
         peer=xor(me,i,groups)
         pltpu.make_async_remote_copy(src_ref=cpack.at[peer],dst_ref=cotarr.at[peer],send_sem=ssem.at[peer],recv_sem=rsem.at[peer],
@@ -131,9 +141,9 @@
     A=pl.BlockSpec(memory_space=pl.ANY)
     sd=jax.ShapeDtypeStruct
     return pl.pallas_call(functools.partial(front_kernel,groups,cap,block),
-      in_specs=[V]*9,out_specs=[V]*9+[A],
-      out_shape=[sd((T,D),BF)]+[sd((D,T),BF)]*4+[sd((H,T),F32),sd((T,D),F32),sd((groups,cap,D),BF),sd((1,T),F32),sd((groups,cap,D),BF)],
-      scratch_shapes=[pltpu.VMEM((groups,cap,D),BF),pltpu.VMEM((T,D),BF),pltpu.SemaphoreType.DMA((groups,)),pltpu.SemaphoreType.DMA((groups,)),pltpu.SemaphoreType.DMA],
+      in_specs=[A]+[V]*4+[A]*4,out_specs=[A]*5+[V]+[A]*2+[V,A],
+      out_shape=[sd((D,T),BF)]*5+[sd((H,T),F32),sd((T,D),F32),sd((groups,cap,D),BF),sd((1,T),F32),sd((groups,cap,D),BF)],
+      scratch_shapes=[pltpu.VMEM((T,D),BF)]+[pltpu.VMEM((D,D),BF)]*4+[pltpu.VMEM((D,T),BF)]*5+[pltpu.VMEM((T,D),F32),pltpu.VMEM((groups,cap,D),BF),pltpu.VMEM((groups,cap,D),BF),pltpu.VMEM((T,D),BF),pltpu.SemaphoreType.DMA((groups,)),pltpu.SemaphoreType.DMA((groups,)),pltpu.SemaphoreType.DMA,pltpu.SemaphoreType.DMA((5,)),pltpu.SemaphoreType.DMA((7,))],
       compiler_params=pltpu.CompilerParams(vmem_limit_bytes=60*2**20,collective_id=0,has_side_effects=True),
       name="front")(tokens,routes_row,cot,g1,g2,wq,wk,wv,wo)
 
@@ -183,8 +193,9 @@
         return pltpu.make_async_remote_copy(src_ref=gst.at[at(j)],dst_ref=gback.at[me],send_sem=gsend.at[i],recv_sem=grecv.at[i],
             device_id={"expert":j},device_id_type=MESH)
     half=groups//2
+    def code(i): return i+(i//half)*((i+half//2)%half+half-i)
     def push(i,c):
-        dispatch(xor(me,i,groups),i).start()
+        dispatch(xor(me,code(i),groups),i).start()
         return c
     lax.fori_loop(half,half+half//2,push,0)
     lax.fori_loop(1,half,push,0)
@@ -196,11 +207,14 @@
     cup.wait(); ccot.wait(); cdown.wait()
     def retcopy(j): return pltpu.make_async_copy(retb,ret.at[j],retsem)
     def actcopy(j): return pltpu.make_async_copy(actb,act.at[at(j)],actsem)
+    def results(j):
+        retb[...]=dot(actb[...],downv[...]).astype(BF)
+        retcopy(j).start()
     def answer(i,c):
-        giveback(xor(me,i,groups),i).start()
+        giveback(xor(me,code(i),groups),i).start()
         return c
     def chunk(i,c):
-        j=xor(me,i,groups)
+        j=xor(me,code(i),groups)
         @pl.when(i==0)
         def _(): own.wait()
         @pl.when(i>0)
@@ -228,16 +242,14 @@
         @pl.when(i==0)
         def _(): pltpu.make_async_copy(gst.at[at(j)],gback.at[me],grecv.at[0]).start()
         actcopy(j).start()
-        @pl.when(i>=1)
+        @pl.when((i>=1)&(i<groups-1))
         def _(): retcopy(j).wait()
-        retb[...]=dot(actb[...],downv[...]).astype(BF)
-        retcopy(j).start()
+        @pl.when(i<groups-1)
+        def _(): results(j)
         return c
     lax.fori_loop(0,groups,chunk,0)
-    retcopy(0).wait()
     actcopy(0).wait()
     def atile(t,b): return pltpu.make_async_copy(act.at[:,pl.ds(pl.multiple_of(t*D,D),D)],downv.at[pl.ds(b*rows,rows)],tsem.at[b])
-    atile(0,0).start(); atile(1,1).start()
     S=512
     steps=F//(2*S)
     def shared(n):
@@ -283,10 +295,11 @@
             if s>=2: tosib(s-2,b).wait_send()
             product(2*s+1-core,place(0,b))
             tosib(s,b).start()
-            if s>=1: finish(s-1)
+            if s>=2: finish(s-1)
             product(2*s+core,place(1,b))
             if n==1 and s+2<steps: atile(s+2,b).start()
-            if s>=1: leave(s-1)
+            if s==0: finish(0)
+            if s!=1: leave(max(s-1,0))
         finish(steps-1)
         for s in range(max(0,steps-2),steps): tosib(s,s%2).wait_send()
         leave(steps-1)
@@ -294,10 +307,14 @@
         return pltpu.make_async_remote_copy(src_ref=chipu.at[s],dst_ref=xgot.at[s],send_sem=xsend.at[s],recv_sem=xrecv.at[s],
             device_id={"replica":across},device_id_type=MESH)
     shared(0)
+    retcopy(0).wait()
+    results(xor(me,code(groups-1),groups))
+    retcopy(0).wait()
+    atile(0,0).start(); atile(1,1).start()
     shared(1)
     pltpu.make_async_copy(gst.at[at(me)],gback.at[me],grecv.at[0]).wait()
     def finish(i,c):
-        j=xor(me,i,groups)
+        j=xor(me,code(i),groups)
         dispatch(j,i).wait_send()
         giveback(j,i).wait()
         return c
@@ -348,12 +365,12 @@
             dqs[i]=part if dqs[i] is None else dqs[i]+part
     return [(x*scale).astype(BF).T for x in dqs],[x.astype(BF) for x in dks],[x.astype(BF) for x in dvs]
 
-def back_kernel(groups,cap,block,early,
+def back_kernel(groups,cap,block,early,tile_at,ret_at,
         gback,ret,slot,hid,cot,tok,normed,q,k,v,att,lse,g1,g2,wq,wk,wv,wo,chipu,chipd,xgot,
         output,gtok,dw,dgain,dup,ddown,rarr,xu,xd,
         vslots,vhid,vcot,vnormed,vq,vk,vv,vatt,vwo,ghl,datt,dq,dk,dv,vgt,dwv,rbuf,gbuf,
         isem,ssem,rsem,lsem,dsend,drecv,osem,xsend,xrecv,fsem,fout,fsend,frecv,gsend,grecv,credit):
-    T,D=vnormed.shape
+    D,T=vnormed.shape
     R=256
     S=chipu.shape[2]
     steps=chipu.shape[0]
@@ -380,15 +397,19 @@
         return pltpu.make_async_remote_copy(src_ref=ret.at[j],dst_ref=rarr.at[me],send_sem=ssem.at[i],recv_sem=rsem.at[i],
             device_id={"expert":j},device_id_type=MESH)
     def push(i,c):
-        send(groups-i).start()
-        return c
-    lax.fori_loop(1,groups,push,0)
+        send(i).start()
+        return c
+    def push_share(p):
+        lax.fori_loop(1+p*(groups-1)//7,1+(p+1)*(groups-1)//7,push,0)
+    for p in range(7):
+        if ret_at[p]<0: push_share(p)
     own=pltpu.make_async_copy(ret.at[me],rarr.at[me],lsem); own.start()
-    def toacross(n,s):
+    def toacross(n,s,p):
         src,dst=(chipu.at[s],xu.at[s-early]) if n==0 else (chipd.at[s],xd.at[s])
-        return pltpu.make_async_remote_copy(src_ref=src,dst_ref=dst,send_sem=xsend.at[n,s],recv_sem=xrecv.at[n,s],
+        m=src.shape[0]//2
+        return pltpu.make_async_remote_copy(src_ref=src.at[pl.ds(p*m,m)],dst_ref=dst.at[pl.ds(p*m,m)],send_sem=xsend.at[n,2*s+p],recv_sem=xrecv.at[n,2*s+p],
             device_id={"replica":across},device_id_type=MESH)
-    late=[(0,s) for s in range(early,steps)]+[(1,s) for s in range(steps)]
+    late=[(n,s,p) for n in range(2) for s in range(0 if n else early,steps) for p in range(2)]
     def spare(n,i):
         return vatt.at[:,pl.ds(i*S,S)] if n==0 else vnormed.at[pl.ds(i*S,S)]
     def finalize(n,s,got):
@@ -413,33 +434,42 @@
     def left(n,s):
         keep,share=leaving(n,s)
         keep.wait(); share.wait_send()
-    for n,s in late[:2]: toacross(n,s).start()
-    bits=[("replica",mine,1)]+[("expert",me,1<<b) for b in range(groups.bit_length()-1)]
-    H=len(bits)
-    base=[0]; other=[]; peers=[]
-    for i,(axis,index,step) in enumerate(bits):
-        n=D>>(i+1)
-        bit=(index//step)%2
-        other.append(base[-1]+(1-bit)*n)
-        base.append(base[-1]+bit*n)
-        peers.append({axis:index+step-2*step*bit})
-    size=[D>>(i+1) for i in range(H)]+[D>>H]
-    offset=[D-(D>>i) for i in range(H+1)]
-    def piece(ref,c,first,n):
-        return ref.at[:,pl.ds(pl.multiple_of(first,n),n),pl.ds(pl.multiple_of(c*W,W),W)]
-    def move(c,k):
+    for i,x in enumerate(late):
+        if tile_at[i]<0: toacross(*x).start()
+    V=W//2
+    half=[(1<<b) for b in range(groups.bit_length()-1)]
+    def partner(index,step): return index+step-2*step*((index//step)%2)
+    paths=[]
+    for steps_of in (half[:-1],half[1::-1]+half[2:-1] if len(half)>2 else half[:-1]):
+        base=[0]; other=[]; peers=[]
+        for i,(axis,index,step) in enumerate([("replica",mine,1)]+[("expert",me,b) for b in steps_of]):
+            n=D>>(i+1)
+            bit=(index//step)%2
+            other.append(base[-1]+(1-bit)*n)
+            base.append(base[-1]+bit*n)
+            peers.append({axis:partner(index,step)})
+        paths.append((base,other,peers))
+    whole=[{"expert":partner(me,half[-1])},{"replica":across}]
+    H=len(paths[0][2])
+    size=[D>>(i+1) for i in range(H)]+[D>>H]*2
+    offset=[D-(D>>i) for i in range(H+1)]+[D]
+    def columns(c,h): return pl.ds(pl.multiple_of(c*W+h*V,V),V)
+    def piece(ref,c,h,first,n):
+        return ref.at[:,pl.ds(pl.multiple_of(first,n),n),columns(c,h)]
+    def move(c,h,k):
+        base,other,peers=paths[h]
         if k<H:
-            src=piece(dwv,c,other[k],size[k]); dst=piece(rbuf,c,offset[k],size[k]); peer=peers[k]
-        elif k==H:
-            src=piece(dwv,c,base[H],size[H]); dst=piece(rbuf,c,offset[H],size[H]); peer={"replica":across}
+            src=piece(dwv,c,h,other[k],size[k]); dst=piece(rbuf,c,h,offset[k],size[k]); peer=peers[k]
+        elif k<H+2:
+            src=piece(dwv,c,h,base[H],size[k]); dst=piece(rbuf,c,h,offset[k],size[k]); peer=whole[k-H]
         else:
-            i=2*H-k
-            src=dst=piece(dwv,c,base[i+1],size[i]); peer=peers[i]
-        return pltpu.make_async_remote_copy(src_ref=src,dst_ref=dst,send_sem=dsend.at[c,k],recv_sem=drecv.at[c,k],device_id=peer,device_id_type=MESH)
-    def gather_in(c,k):
-        first=base[min(k+1,H)]; n=size[k]
+            i=2*H+1-k
+            src=dst=piece(dwv,c,h,base[i+1],size[i]); peer=peers[i]
+        return pltpu.make_async_remote_copy(src_ref=src,dst_ref=dst,send_sem=dsend.at[2*c+h,k],recv_sem=drecv.at[2*c+h,k],device_id=peer,device_id_type=MESH)
+    def gather_in(c,h,k):
+        first=paths[h][0][min(k+1,H)]; n=size[k]
         m=min(n,64)
-        cols=pl.ds(pl.multiple_of(c*W,W),W)
+        cols=columns(c,h)
         def add(i,z):
             r=pl.ds(pl.multiple_of(first+i*m,m),m)
             o=pl.ds(pl.multiple_of(offset[k]+i*m,m),m)
@@ -450,20 +480,22 @@
     def out_dense(c):
         cols=pl.ds(pl.multiple_of(c*W,W),W)
         return pltpu.make_async_copy(dwv.at[:,:,cols],dw.at[:,:,cols],osem.at[c])
-    K=2*H+2
+    K=2*H+3
+    last=parts+K-1
     def progress(t):
-        for k in range(K-1,-1,-1):
+        for k in [x for x in range(K-1,-1,-1) if x!=H+2]+[H+2]:
             c=t-k
             @pl.when((c>=0)&(c<parts))
             def _():
-                if k>0:
-                    move(c,k-1).wait()
-                    if k<=H: pl.semaphore_signal(credit.at[c,k-1],inc=1,device_id=peers[k-1],device_id_type=MESH)
-                if 0<k<=H+1: gather_in(c,k-1)
-                if H<k<K-1: pl.semaphore_wait(credit.at[c,2*H-k],1)
-                if k<K-1: move(c,k).start()
-                else: out_dense(c).start()
-    gbits=peers+[{"replica":across}]
+                for h in range(2):
+                    if k>0:
+                        move(c,h,k-1).wait()
+                        if k<=H: pl.semaphore_signal(credit.at[2*c+h,k-1],inc=1,device_id=paths[h][2][k-1],device_id_type=MESH)
+                    if 0<k<=H+2: gather_in(c,h,k-1)
+                    if H+2<=k<K-1: pl.semaphore_wait(credit.at[2*c+h,2*H+1-k],1)
+                    if k<K-1: move(c,h,k).start()
+                if k==K-1: out_dense(c).start()
+    gbits=paths[0][2]+whole
     def gain_move(j):
         return pltpu.make_async_remote_copy(src_ref=dgain,dst_ref=gbuf.at[j],send_sem=gsend.at[j],recv_sem=grecv.at[j],device_id=gbits[j],device_id_type=MESH)
     def gain_step(j):
@@ -519,10 +551,10 @@
             cols=pl.ds(pl.multiple_of(t*W,W),W)
             for n,x in enumerate((dq,dk,dv)):
                 def rowpart(i,c):
-                    s=pl.ds(pl.multiple_of(i*R,R),R)
-                    dwv[n,s,cols]=dg(vnormed[:,s],x[:,cols],0,0).astype(BF)
+                    s=pl.ds(pl.multiple_of(i*2*R,2*R),2*R)
+                    dwv[n,s,cols]=dot(vnormed[s,:],x[:,cols]).astype(BF)
                     return c
-                lax.fori_loop(0,D//R,rowpart,0)
+                lax.fori_loop(0,D//(2*R),rowpart,0)
         @pl.when(t==parts-1)
         def _():
             for x in loads: x.start()
@@ -540,12 +572,20 @@
             dgain[0:1,:]+=jnp.sum(gn*u,axis=0,keepdims=True)
             vgt[r,:]+=inv*(m-jnp.mean(m,axis=-1,keepdims=True)-u*jnp.mean(m*u,axis=-1,keepdims=True))
         progress(t)
-        for i,at in ((2,1),(4,4)):
-            @pl.when(t==at)
-            def _():
-                for n,s in late[i:i+2]: toacross(n,s).start()
+        for at in range(last):
+            if at in tile_at or at in ret_at:
+                @pl.when(t==at)
+                def _():
+                    for i,x in enumerate(late):
+                        if tile_at[i]==at: toacross(*x).start()
+                    for p in range(7):
+                        if ret_at[p]==at: push_share(p)
         @pl.when(t==2*parts)
         def _(): pltpu.make_async_copy(vgt,gtok,isem.at[0]).start()
+        @pl.when(t==2*parts)
+        def _(): returned()
+        @pl.when((t>=2*parts)&(t<3*parts))
+        def _(): final(t-2*parts)
         for j in range(ingain):
             @pl.when(t==2*parts+j)
             def _(): gain_step(j)
@@ -553,6 +593,17 @@
             @pl.when(t==parts+1+p)
             def _(): settle(p)
         return c
+    def returned():
+        own.wait()
+        def finish(i,c):
+            send(i).wait()
+            return c
+        lax.fori_loop(1,groups,finish,0)
+        load=pltpu.make_async_copy(rarr,vslots,lsem); load.start(); load.wait()
+    def final(i):
+        n=T//parts
+        r=pl.ds(pl.multiple_of(i*n,n),n)
+        ghl[r,:]=(vhid[r,:]+gathered(r)).astype(BF)
     order=[(0,s) for s in range(steps)]+[(1,s) for s in range(steps)]
     def settle(p):
         n,s=order[p]
@@ -560,28 +611,14 @@
         if n==0 and s<early:
             finalize(n,s,xgot.at[s])
         else:
-            toacross(n,s).wait()
+            for i in range(2): toacross(n,s,i).wait()
             finalize(n,s,xu.at[s-early] if n==0 else xd.at[s])
         if p>0 and order[p-1][0]!=n: left(*order[p-1])
-    last=parts+K-1
     inloop=steps+steps//2
     ingain=min(len(gbits)+1,last-2*parts)
-    for n,s in late[6:]: toacross(n,s).start()
     lax.fori_loop(0,last,time,0)
     for j in range(ingain,len(gbits)+1): gain_step(j)
-    own.wait()
-    def finish(i,c):
-        send(i).wait()
-        return c
-    lax.fori_loop(1,groups,finish,0)
-    load=pltpu.make_async_copy(rarr,vslots,lsem); load.start()
     for p in range(inloop,len(order)): settle(p)
-    load.wait()
-    def final(i,c):
-        r=pl.ds(pl.multiple_of(i*R,R),R)
-        ghl[r,:]=(vhid[r,:]+gathered(r)).astype(BF)
-        return c
-    lax.fori_loop(0,T//R,final,0)
     last_out=pltpu.make_async_copy(ghl,output,isem.at[1]); last_out.start()
     left(*order[-1])
     for n,s in order: leaving(n,s)[1].wait_recv()
@@ -589,28 +626,54 @@
     pltpu.make_async_copy(vgt,gtok,isem.at[0]).wait()
     last_out.wait()
 
-def back(gback,ret,slot,hid,cot,tok,normed,q,k,v,att,lse,g1,g2,wq,wk,wv,wo,chipu,chipd,xgot,block=256):
+def back(gback,ret,slot,hid,cot,tok,normed,q,k,v,att,lse,g1,g2,wq,wk,wv,wo,chipu,chipd,xgot,tile_at,ret_at,block=256):
     groups,cap,D=ret.shape
     T=tok.shape[0]
     steps,_,S=chipu.shape
     early=xgot.shape[0]
     F=2*steps*S
-    H=groups.bit_length()
+    H=groups.bit_length()-1
     V=pl.BlockSpec(memory_space=pltpu.VMEM)
     A=pl.BlockSpec(memory_space=pl.ANY)
     sd=jax.ShapeDtypeStruct
     DMA=pltpu.SemaphoreType.DMA
     M=lambda *s: pltpu.VMEM(s,BF)
-    return pl.pallas_call(functools.partial(back_kernel,groups,cap,block,early),
+    return pl.pallas_call(functools.partial(back_kernel,groups,cap,block,early,tile_at,ret_at),
       in_specs=[A,A,V]+[A]*8+[V]*3+[A]*7,out_specs=[A]*3+[V]+[A]*5,
       out_shape=[sd((T,D),BF),sd((T,D),F32),sd((4,D,D),BF),sd((8,D),F32),sd((D,F),BF),sd((F,D),BF),sd((groups,cap,D),BF),
          sd((steps-early,D,S),BF),sd((steps,S,D),BF)],
-      scratch_shapes=[M(groups,cap,D),pltpu.VMEM((T,D),F32),M(T,D),M(T,D),M(D,T),M(D,T),M(D,T),M(D,T),M(D,D),M(T,D),M(D,T),M(T,D),M(T,D),M(T,D),
-         pltpu.VMEM((T,D),F32),M(4,D,D),M(4,D,D),pltpu.VMEM((H+1,8,D),F32),
-         DMA((9,)),DMA((groups,)),DMA((groups,)),DMA,DMA((4,2*H+1)),DMA((4,2*H+1)),DMA((4,)),DMA((2,steps)),DMA((2,steps)),DMA((2,)),DMA((2,)),DMA((2,steps)),DMA((2,steps)),
-         DMA((H+1,)),DMA((H+1,)),pltpu.SemaphoreType.REGULAR((4,H))],
+      scratch_shapes=[M(groups,cap,D),pltpu.VMEM((T,D),F32),M(T,D),M(D,T),M(D,T),M(D,T),M(D,T),M(D,T),M(D,D),M(T,D),M(D,T),M(T,D),M(T,D),M(T,D),
+         pltpu.VMEM((T,D),F32),M(4,D,D),M(4,D+(D>>H),D),pltpu.VMEM((H+2,8,D),F32),
+         DMA((9,)),DMA((groups,)),DMA((groups,)),DMA,DMA((8,2*H+2)),DMA((8,2*H+2)),DMA((4,)),DMA((2,2*steps)),DMA((2,2*steps)),DMA((2,)),DMA((2,)),DMA((2,steps)),DMA((2,steps)),
+         DMA((H+2,)),DMA((H+2,)),pltpu.SemaphoreType.REGULAR((8,H))],
       compiler_params=pltpu.CompilerParams(vmem_limit_bytes=63*2**20+2**19,collective_id=2,has_side_effects=True),
       name="back")(gback,ret,slot,hid,cot,tok,normed,q,k,v,att,lse,g1,g2,wq,wk,wv,wo,chipu,chipd,xgot)
+
+
+def widen_kernel(dup,ddown,dw,output,gtok,gup,gdown,*rest):
+    gup[...]=dup[...].astype(F32)
+    gdown[...]=ddown[...].astype(F32)
+    for i in range(4): rest[i][...]=dw[i].astype(F32)
+    rest[4][...]=output[...]
+    rest[5][...]=gtok[...]
+
+
+def widen(dup,ddown,dw,output,gtok,count=4):
+    T,D=output.shape
+    F=dup.shape[1]
+    n=D//count
+    rows=lambda r,c: pl.BlockSpec((r,c),lambda i:(i,0))
+    sd=jax.ShapeDtypeStruct
+    return pl.pallas_call(widen_kernel,grid=(count,),
+        in_specs=[rows(n,F),rows(F//count,D),pl.BlockSpec((4,n,D),lambda i:(0,i,0)),rows(T//count,D),rows(T//count,D)],
+        out_specs=[rows(n,F),rows(F//count,D)]+[rows(n,D)]*4+[rows(T//count,D)]*2,
+        out_shape=[sd((D,F),F32),sd((F,D),F32)]+[sd((D,D),F32)]*4+[sd((T,D),BF),sd((T,D),F32)],
+        compiler_params=pltpu.CompilerParams(vmem_limit_bytes=60*2**20),name="widen")(dup,ddown,dw,output,gtok)
+
+
+EARLY=3
+TILE_AT=(-1,-1,0,1,2,3,4,6,8,9)
+RET_AT=(-1,-1,-1,-1,0,1,2)
 
 
 def per_device(tokens,routes,gain_one,query_weight,key_weight,value_weight,out_weight,gain_two,up_weight,down_weight,cotangent):
@@ -620,10 +683,12 @@
     g1=gain_one.reshape(1,D); g2=gain_two.reshape(1,D)
     weights=(query_weight,key_weight,value_weight,out_weight)
     normed,q,k,v,att,lse,hid,pack,slot,cotarr=front(tokens,routes.reshape(1,T),cotangent,g1,g2,*weights,groups,cap)
-    gback,ret,chipu,chipd,xgot,_=expert(pack,cotarr,up_weight[0],down_weight[0],2)
-    output,gtok,dw,dgain,dup,ddown,_,_,_=back(gback,ret,slot,hid,cotangent,tokens,normed,q,k,v,att,lse,g1,g2,*weights,chipu,chipd,xgot)
-    ws=[dw[i].astype(F32) for i in range(4)]
-    return (output,gtok,dgain[0],*ws,dgain[1],dup.astype(F32)[None],ddown.astype(F32)[None])
+    gback,ret,chipu,chipd,xgot,_=expert(pack,cotarr,up_weight[0],down_weight[0],EARLY)
+    output,gtok,dw,dgain,dup,ddown,_,_,_=back(gback,ret,slot,hid,cotangent,tokens,normed,q,k,v,att,lse,g1,g2,*weights,chipu,chipd,xgot,TILE_AT,RET_AT)
+    gup,gdown,gq,gk,gv,go,output,gtok=widen(dup,ddown,dw,output,gtok)
+    return (output,gtok,dgain[0],gq,gk,gv,go,dgain[1],gup[None],gdown[None])
+
+
 def solution(mesh):
     rows=P(("expert","replica"),None)
     each=P("expert",None,None)

time: 605 us -> 560 us (0.926)
  other arithmetic: 33.8 us -> 0 us
    broadcast_in_dim x2 -> x0, other arithmetic: 23.5 us -> none  [the longest x1 11.8 us: per_device(): dup.astype(F32)[None]]
    pallas_call x1, Pallas kernels: 186 us -> 205 us  [expert(): pl.pallas_call(functools.partial(expert_kernel, groups, cap, early), in_s...]
    pallas_call x1 -> x2, Pallas kernels: 252 us -> 236 us  [the longest x1 208 us: back(): pl.pallas_call(functools.partial(back_kernel, groups, cap, block, early,...]
    convert_element_type x1 -> x0, other arithmetic: 10.3 us -> none  [per_device(): ws = [dw[i].astype(F32) for i in range(4)]]
    pallas_call x1, Pallas kernels: 118 us -> 109 us  [front(): pl.pallas_call(functools.partial(front_kernel, groups, cap, block), in_sp...]
where the time goes in v3:
time: 560 us; the launch traced here: 552 us
  Pallas kernels  549 us (98%)
    pallas_call x1, Pallas kernels, back(): pl.pallas_call(functools.partial(back_kernel, groups, cap, block, early,...  208 us
    pallas_call x1, Pallas kernels, expert(): pl.pallas_call(functools.partial(expert_kernel, groups, cap, early), in_s...  205 us
    pallas_call x1, Pallas kernels, front(): pl.pallas_call(functools.partial(front_kernel, groups, cap, block), in_sp...  109 us
    pallas_call x1, Pallas kernels, widen(): pl.pallas_call(widen_kernel, grid=(count,), in_specs=[rows(n, F), rows(F...  27.3 us

profile of v3, /device:TPU:0, one launch (start us, length us, event | category | flops | bytes accessed | tf_op | source)
XLA Modules:
  0.0 551.7 jit_solution(2266107418608956704)
XLA Ops:
  0.6 108.7 %front.1 = (bf16[1024,1024]{1,0:T(8,128)(2,1)}, bf16[1024,1024]{1,0:T(8,128)(2,1)}, bf16[1024,1024]{1,0:T(8,128)(2,1)}, bf16[1024,1024]{1,0:T(8,128)(2,1)}, bf16...) custom-call(bf16[1024,1024]{1,0:T(8,128)(2,1)} %tok.1, ...), custom_call_target="tpu_custom_call" | custom-call | tf_op jit(solution)/shard_map/front/pallas_call | solution.py:143
  109.4 204.6 %experts.1 = (bf16[8,256,1024]{2,1,0:T(8,128)(2,1)}, bf16[8,256,1024]{2,1,0:T(8,128)(2,1)}, bf16[4,1024,512]{2,1,0:T(8,128)(2,1)}, bf16[4,512,1024]{2,1,0:T(8,12...) custom-call(bf16[8,256,1024]{2,1,0:T(8,128)(2,1)} %get-tuple-element.39.pack, ...), custom_call_target="tpu_custom_call" | custom-call | tf_op jit(solution)/shard_map/experts/pallas_call | solution.py:332
  314.0 208.5 %back.1 = (bf16[1024,1024]{1,0:T(8,128)(2,1)}, f32[1024,1024]{1,0:T(8,128)}, bf16[4,1024,1024]{2,1,0:T(8,128)(2,1)}, f32[8,1024]{1,0:T(8,128)}, bf16[1024,4096]{...) custom-call(bf16[8,256,1024]{2,1,0:T(8,128)(2,1)} %get-tuple-element, ...), custom_call_target="tpu_custom_call" | custom-call | tf_op jit(solution)/shard_map/back/pallas_call | solution.py:641
  522.5 1.4 fusion
  523.9 27.3 %widen.1 = (f32[1024,4096]{1,0:T(8,128)}, f32[4096,1024]{1,0:T(8,128)}, f32[1024,1024]{1,0:T(8,128)}, f32[1024,1024]{1,0:T(8,128)}, f32[1024,1024]{1,0:T(8,128)}...) custom-call(bf16[1024,4096]{1,0:T(8,128)(2,1)} %get-tuple-element.54.dup, ...), custom_call_target="tpu_custom_call" | custom-call | tf_op jit(solution)/shard_map/widen/pallas_call | solution.py:667

commit v4 on v3

--- a/solution.py
+++ b/solution.py
@@ -455,7 +455,7 @@
     offset=[D-(D>>i) for i in range(H+1)]+[D]
     def columns(c,h): return pl.ds(pl.multiple_of(c*W+h*V,V),V)
     def piece(ref,c,h,first,n):
-        return ref.at[:,pl.ds(pl.multiple_of(first,n),n),columns(c,h)]
+        return ref.at[2*c+h,:,pl.ds(pl.multiple_of(first,n),n),:]
     def move(c,h,k):
         base,other,peers=paths[h]
         if k<H:
@@ -469,17 +469,16 @@
     def gather_in(c,h,k):
         first=paths[h][0][min(k+1,H)]; n=size[k]
         m=min(n,64)
-        cols=columns(c,h)
+        lane=2*c+h
         def add(i,z):
             r=pl.ds(pl.multiple_of(first+i*m,m),m)
             o=pl.ds(pl.multiple_of(offset[k]+i*m,m),m)
             for x in range(4):
-                dwv[x,r,cols]=(dwv[x,r,cols].astype(F32)+rbuf[x,o,cols].astype(F32)).astype(BF)
+                dwv[lane,x,r,:]=(dwv[lane,x,r,:].astype(F32)+rbuf[lane,x,o,:].astype(F32)).astype(BF)
             return z
         lax.fori_loop(0,n//m,add,0)
-    def out_dense(c):
-        cols=pl.ds(pl.multiple_of(c*W,W),W)
-        return pltpu.make_async_copy(dwv.at[:,:,cols],dw.at[:,:,cols],osem.at[c])
+    def out_dense(c,h):
+        return pltpu.make_async_copy(dwv.at[2*c+h],dw.at[:,:,columns(c,h)],osem.at[2*c+h])
     K=2*H+3
     last=parts+K-1
     def progress(t):
@@ -494,7 +493,7 @@
                     if 0<k<=H+2: gather_in(c,h,k-1)
                     if H+2<=k<K-1: pl.semaphore_wait(credit.at[2*c+h,2*H+1-k],1)
                     if k<K-1: move(c,h,k).start()
-                if k==K-1: out_dense(c).start()
+                    if k==K-1: out_dense(c,h).start()
     gbits=paths[0][2]+whole
     def gain_move(j):
         return pltpu.make_async_remote_copy(src_ref=dgain,dst_ref=gbuf.at[j],send_sem=gsend.at[j],recv_sem=grecv.at[j],device_id=gbits[j],device_id_type=MESH)
@@ -525,7 +524,8 @@
     def outproj(i,c):
         s=pl.ds(pl.multiple_of(i*R,R),R)
         datt[s,:]=dg(vwo[s,:],ghl[...],1,1).astype(BF)
-        dwv[3,s,:]=dot(vatt[s,:],ghl[...]).astype(BF)
+        full=dot(vatt[s,:],ghl[...]).astype(BF)
+        for x in range(2*parts): dwv[x,3,s,:]=full[:,x*V:(x+1)*V]
         return c
     lax.fori_loop(0,D//R,outproj,0)
     for c in copies[5:]: c.wait()
@@ -552,7 +552,8 @@
             for n,x in enumerate((dq,dk,dv)):
                 def rowpart(i,c):
                     s=pl.ds(pl.multiple_of(i*2*R,2*R),2*R)
-                    dwv[n,s,cols]=dot(vnormed[s,:],x[:,cols]).astype(BF)
+                    full=dot(vnormed[s,:],x[:,cols]).astype(BF)
+                    for h in range(2): dwv[2*t+h,n,s,:]=full[:,h*V:(h+1)*V]
                     return c
                 lax.fori_loop(0,D//(2*R),rowpart,0)
         @pl.when(t==parts-1)
@@ -587,10 +588,10 @@
         @pl.when((t>=2*parts)&(t<3*parts))
         def _(): final(t-2*parts)
         for j in range(ingain):
-            @pl.when(t==2*parts+j)
+            @pl.when(t==2*parts-1+j)
             def _(): gain_step(j)
         for p,(n,s) in enumerate(order[:inloop]):
-            @pl.when(t==parts+1+p)
+            @pl.when(t==parts+p)
             def _(): settle(p)
         return c
     def returned():
@@ -614,15 +615,16 @@
             for i in range(2): toacross(n,s,i).wait()
             finalize(n,s,xu.at[s-early] if n==0 else xd.at[s])
         if p>0 and order[p-1][0]!=n: left(*order[p-1])
-    inloop=steps+steps//2
-    ingain=min(len(gbits)+1,last-2*parts)
+    inloop=min(2*steps,last-parts)
+    ingain=min(len(gbits)+1,last-2*parts+1)
     lax.fori_loop(0,last,time,0)
     for j in range(ingain,len(gbits)+1): gain_step(j)
     for p in range(inloop,len(order)): settle(p)
     last_out=pltpu.make_async_copy(ghl,output,isem.at[1]); last_out.start()
     left(*order[-1])
     for n,s in order: leaving(n,s)[1].wait_recv()
-    for c in range(parts): out_dense(c).wait()
+    for c in range(parts):
+        for h in range(2): out_dense(c,h).wait()
     pltpu.make_async_copy(vgt,gtok,isem.at[0]).wait()
     last_out.wait()
 
@@ -643,8 +645,8 @@
       out_shape=[sd((T,D),BF),sd((T,D),F32),sd((4,D,D),BF),sd((8,D),F32),sd((D,F),BF),sd((F,D),BF),sd((groups,cap,D),BF),
          sd((steps-early,D,S),BF),sd((steps,S,D),BF)],
       scratch_shapes=[M(groups,cap,D),pltpu.VMEM((T,D),F32),M(T,D),M(D,T),M(D,T),M(D,T),M(D,T),M(D,T),M(D,D),M(T,D),M(D,T),M(T,D),M(T,D),M(T,D),
-         pltpu.VMEM((T,D),F32),M(4,D,D),M(4,D+(D>>H),D),pltpu.VMEM((H+2,8,D),F32),
-         DMA((9,)),DMA((groups,)),DMA((groups,)),DMA,DMA((8,2*H+2)),DMA((8,2*H+2)),DMA((4,)),DMA((2,2*steps)),DMA((2,2*steps)),DMA((2,)),DMA((2,)),DMA((2,steps)),DMA((2,steps)),
+         pltpu.VMEM((T,D),F32),M(8,4,D,D//8),M(8,4,D+(D>>H),D//8),pltpu.VMEM((H+2,8,D),F32),
+         DMA((9,)),DMA((groups,)),DMA((groups,)),DMA,DMA((8,2*H+2)),DMA((8,2*H+2)),DMA((8,)),DMA((2,2*steps)),DMA((2,2*steps)),DMA((2,)),DMA((2,)),DMA((2,steps)),DMA((2,steps)),
          DMA((H+2,)),DMA((H+2,)),pltpu.SemaphoreType.REGULAR((8,H))],
       compiler_params=pltpu.CompilerParams(vmem_limit_bytes=63*2**20+2**19,collective_id=2,has_side_effects=True),
       name="back")(gback,ret,slot,hid,cot,tok,normed,q,k,v,att,lse,g1,g2,wq,wk,wv,wo,chipu,chipd,xgot)
@@ -672,8 +674,8 @@
 
 
 EARLY=3
-TILE_AT=(-1,-1,0,1,2,3,4,6,8,9)
-RET_AT=(-1,-1,-1,-1,0,1,2)
+TILE_AT=(-1,-1,0,1,2,3,5,6,7,8)
+RET_AT=(-1,-1,-1,0,1,3,5)
 
 
 def per_device(tokens,routes,gain_one,query_weight,key_weight,value_weight,out_weight,gain_two,up_weight,down_weight,cotangent):

time: 560 us -> 550 us (0.982)
  Pallas kernels: 549 us -> 539 us
    pallas_call x1, Pallas kernels: 208 us -> 199 us  [back(): pl.pallas_call(functools.partial(back_kernel, groups, cap, block, early,...]
where the time goes in v4:
time: 550 us; the launch traced here: 542 us
  Pallas kernels  539 us (98%)
    pallas_call x1, Pallas kernels, expert(): pl.pallas_call(functools.partial(expert_kernel, groups, cap, early), in_s...  205 us
    pallas_call x1, Pallas kernels, back(): pl.pallas_call(functools.partial(back_kernel, groups, cap, block, early,...  199 us
    pallas_call x1, Pallas kernels, front(): pl.pallas_call(functools.partial(front_kernel, groups, cap, block), in_sp...  109 us
    pallas_call x1, Pallas kernels, widen(): pl.pallas_call(widen_kernel, grid=(count,), in_specs=[rows(n, F), rows(F...  27.3 us

profile of v4, /device:TPU:0, one launch (start us, length us, event | category | flops | bytes accessed | tf_op | source)
XLA Modules:
  0.0 541.9 jit_solution(2831825226636563272)
XLA Ops:
  0.6 108.7 %front.1 = (bf16[1024,1024]{1,0:T(8,128)(2,1)}, bf16[1024,1024]{1,0:T(8,128)(2,1)}, bf16[1024,1024]{1,0:T(8,128)(2,1)}, bf16[1024,1024]{1,0:T(8,128)(2,1)}, bf16...) custom-call(bf16[1024,1024]{1,0:T(8,128)(2,1)} %tok.1, ...), custom_call_target="tpu_custom_call" | custom-call | tf_op jit(solution)/shard_map/front/pallas_call | solution.py:143
  109.4 204.6 %experts.1 = (bf16[8,256,1024]{2,1,0:T(8,128)(2,1)}, bf16[8,256,1024]{2,1,0:T(8,128)(2,1)}, bf16[4,1024,512]{2,1,0:T(8,128)(2,1)}, bf16[4,512,1024]{2,1,0:T(8,12...) custom-call(bf16[8,256,1024]{2,1,0:T(8,128)(2,1)} %get-tuple-element.39.pack, ...), custom_call_target="tpu_custom_call" | custom-call | tf_op jit(solution)/shard_map/experts/pallas_call | solution.py:332
  314.0 198.7 %back.1 = (bf16[1024,1024]{1,0:T(8,128)(2,1)}, f32[1024,1024]{1,0:T(8,128)}, bf16[4,1024,1024]{2,1,0:T(8,128)(2,1)}, f32[8,1024]{1,0:T(8,128)}, bf16[1024,4096]{...) custom-call(bf16[8,256,1024]{2,1,0:T(8,128)(2,1)} %get-tuple-element, ...), custom_call_target="tpu_custom_call" | custom-call | tf_op jit(solution)/shard_map/back/pallas_call | solution.py:643
  512.8 1.4 fusion
  514.2 27.3 %widen.1 = (f32[1024,4096]{1,0:T(8,128)}, f32[4096,1024]{1,0:T(8,128)}, f32[1024,1024]{1,0:T(8,128)}, f32[1024,1024]{1,0:T(8,128)}, f32[1024,1024]{1,0:T(8,128)}...) custom-call(bf16[1024,4096]{1,0:T(8,128)(2,1)} %get-tuple-element.54.dup, ...), custom_call_target="tpu_custom_call" | custom-call | tf_op jit(solution)/shard_map/widen/pallas_call | solution.py:669
